TPU v7x, 1024 devices: a whole 8x8x8 slice. The times are simulated.
1024 devices in a mesh: dp: 2 (over core), node: 64 (over y, x), chip: 8 (over z).
Axes of the slice: x: 8, y: 8, z: 8, core: 2. Of those that a mesh axis runs over, the one named last changes fastest.
Arguments:
- tokens: bfloat16 [8192, 2560], P(('dp', 'chip')), may hold values from -6 to 6
- slot_token: int32 [2, 8, 64, 16], P('dp', 'chip'), may hold values from 0 to 512, as said below
- grad_act: bfloat16 [256, 327680], P(None, ('dp', 'node', 'chip')), may hold values from -6 to 6
- w_up: bfloat16 [2560, 327680], P(None, ('dp', 'node', 'chip')), may hold values from -0.125 to 0.125
Outputs:
- grad_w_up: bfloat16 [2560, 327680], P(None, ('dp', 'node', 'chip'))
- grad_x: float32 [8192, 2560], P(('dp', 'chip'), 'node')
Inputs may be any that keep to these rules, and one draw needn't show every extreme that they name: slot_token[s, c, e, m] indexes a token within the 512 rows of token shard (s, c); 512 marks an empty slot. Each block of 16 slots holds 1 to 16 distinct tokens first and then empty slots; some blocks of every expert are full.
All inputs are finite; a program needn't handle non-finite values.
Results may differ from a plain program's by a relative error of at most 0.015.
Values may be sent and summed in bfloat16 or wider, within the bound.
No kernel may reach another device: no remote copies, remote signals or barrier semaphores. Data moves between devices by JAX's collectives and lax.ppermute only.
A program may use at most 32 MiB of HBM per device.

v0:
```python
import jax
import jax.numpy as jnp
from jax import lax
from jax.sharding import PartitionSpec as P


def gelu_slope(value):
    scale = 0.7978845608
    cubic = 0.044715
    inner = jnp.tanh(scale * (value + cubic * value * value * value))
    return 0.5 * (1.0 + inner) + 0.5 * value * (1.0 - inner * inner) * scale * (
        1.0 + 3.0 * cubic * value * value
    )


def spread_rows(onehot, returned):
    return jnp.einsum(
        "dmt,dmk->tk", onehot.astype(jnp.float32), returned, precision=lax.Precision.HIGHEST
    )


def body(tokens, slot_token, grad_act, w_up):
    tok_grp, width = tokens.shape
    n_data = lax.axis_size("dp")
    n_nodes = lax.axis_size("node")
    node = lax.axis_index("node")
    depth = slot_token.shape[3]
    lists = slot_token[0, 0].reshape(n_data, n_nodes // 2, depth)
    chosen = lax.dynamic_index_in_dim(lists, node // 2, 1, keepdims=False)
    onehot = chosen[:, :, None] == jnp.arange(tok_grp, dtype=jnp.int32)[None, None, :]
    picked = jnp.einsum(
        "dmt,tk->dmk", onehot.astype(jnp.bfloat16), tokens, preferred_element_type=jnp.float32
    ).astype(jnp.bfloat16)
    arrived = lax.all_to_all(picked, "dp", split_axis=0, concat_axis=0, tiled=True)
    count = n_data * depth
    gathered = lax.all_gather(arrived.reshape(count, width), "chip", axis=0, tiled=True)
    pre = jnp.dot(gathered, w_up, preferred_element_type=jnp.float32)
    dh = (grad_act.astype(jnp.float32) * gelu_slope(pre)).astype(jnp.bfloat16)
    grad_w_up = lax.dot_general(
        gathered, dh, (((0,), (0,)), ((), ())), preferred_element_type=jnp.float32
    ).astype(jnp.bfloat16)
    summed = lax.psum_scatter(
        lax.dot_general(
            dh, w_up, (((1,), (1,)), ((), ())), preferred_element_type=jnp.float32
        ).astype(jnp.bfloat16),
        "chip",
        scatter_dimension=0,
        tiled=True,
    ).astype(jnp.float32)
    rows_back = lax.all_to_all(
        summed.reshape(n_data, depth, width).astype(jnp.bfloat16),
        "dp",
        split_axis=0,
        concat_axis=0,
        tiled=True,
    ).astype(jnp.float32)
    contrib = spread_rows(onehot, rows_back)
    grad_x = lax.psum_scatter(contrib, "node", scatter_dimension=1, tiled=True)
    return (grad_w_up, grad_x)


def solution(mesh):
    placed = (
        P(("dp", "chip"), None),
        P("dp", "chip", None, None),
        P(None, ("dp", "node", "chip")),
        P(None, ("dp", "node", "chip")),
    )
    return jax.shard_map(
        body,
        mesh=mesh,
        in_specs=placed,
        out_specs=(P(None, ("dp", "node", "chip")), P(("dp", "chip"), "node")),
        check_vma=False,
    )
```

profile of v0, /device:TPU:1, one launch (start us, length us, event | category | flops | bytes accessed | tf_op | source)
XLA Modules:
  0.0 383.1 jit_solution(1052796922013883613)
XLA Ops:
  7.2 0.0 copy-start
  7.2 0.0 all-gather.2.cloned.1.call-start
  7.2 0.9 reshape_squeeze.3
  8.2 0.1 constant_dynamic-slice_fusion
  8.2 0.1 copy.8
  8.3 0.6 copy-done
  8.9 0.6 convolution_convert_fusion.2
  9.5 18.4 %all_to_all.10 = bf16[2,16,2560]{2,1,0:T(8,128)(2,1)} all-to-all(bf16[2,16,2560]{2,1,0:T(8,128)(2,1)S(1)} %convolution_convert_fusion.2), channel_id=1, replica_groups=mesh['dp'=2,'node'=64,'chip'=8] {'dp'}, dimensions={0} | all-to-all | bytes 327680 | tf_op jit(solution)/shard_map/all_to_all | solution.py:34
  27.9 0.0 all-gather.2.cloned.1.call-update
  27.9 0.0 copy-start.2
  27.9 0.0 reduce-scatter.5.cloned.1.call-start
  28.0 41.0 %all-gather.2.cloned.1.call-done = bf16[256,2560]{1,0:T(8,128)(2,1)} async-done(((bf16[32,2560]{1,0:T(8,128)(2,1)}), bf16[256,2560]{1,0:T(8,128)(2,1)}) %all-gather.2.cloned.1.call-update) | async-done | bytes 1310736 | tf_op jit(solution)/shard_map/all_gather | solution.py:36
  68.9 0.0 copy-start.1
  68.9 2.6 fusion.34
  71.5 0.0 copy-done.2
  71.5 0.0 copy-done.1
  71.5 2.1 convolution_convert_fusion.1
  73.6 0.0 reduce-scatter.5.cloned.1.call-update
  73.6 0.0 reduce-scatter.7.cloned.1.call-start
  73.7 44.2 %reduce-scatter.5.cloned.1.call-done = bf16[32,2560]{1,0:T(8,128)(2,1)} async-done(((bf16[256,2560]{1,0:T(8,128)(2,1)}), bf16[32,2560]{1,0:T(8,128)(2,1)}) %reduce-scatter.5.cloned.1.call-update) | async-done | bytes 163856 | tf_op jit(solution)/shard_map/reduce_scatter | solution.py:42
  117.9 9.6 %all_to_all.11 = bf16[2,16,2560]{2,1,0:T(8,128)(2,1)S(1)} all-to-all(bf16[2,16,2560]{2,1,0:T(8,128)(2,1)} %bitcast.19), channel_id=1, replica_groups=mesh['dp'=2,'node'=64,'chip'=8] {'dp'}, dimensions={0} | all-to-all | bytes 327680 | tf_op jit(solution)/shard_map/all_to_all | solution.py:50
  127.5 3.2 convolution_bitcast_fusion
  130.7 0.0 reduce-scatter.7.cloned.1.call-update
  130.7 3.2 convolution_convert_fusion
  133.9 242.7 %reduce-scatter.7.cloned.1.call-done = f32[512,40]{0,1:T(8,128)} async-done(((f32[512,2560]{0,1:T(8,128)}), f32[512,40]{0,1:T(8,128)}) %reduce-scatter.7.cloned.1.call-update) | async-done | bytes 81936
Async XLA Ops:
  7.2 1.8 copy-start
  7.2 61.7 %all-gather.2.cloned.1.call-start = ((), (), s32[]{:S(2)}) async-start(), calls=%async_computation.4 | async-start | bytes 1474560 | tf_op jit(solution)/shard_map/all_gather | solution.py:36
  27.9 43.6 %copy-start.2 = (bf16[256,320]{0,1:T(8,128)(2,1)S(1)}, bf16[256,320]{0,1:T(8,128)(2,1)}, u32[]{:S(2)}) copy-start(bf16[256,320]{0,1:T(8,128)(2,1)} %param.6) | copy-start | bytes 491524
  27.9 89.9 %reduce-scatter.5.cloned.1.call-start = ((), (), s32[]{:S(2)}) async-start(), calls=%async_computation.5 | async-start | bytes 1474560 | tf_op jit(solution)/shard_map/reduce_scatter | solution.py:42
  68.9 2.6 copy-start.1
  73.6 303.0 %reduce-scatter.7.cloned.1.call-start = ((), (), s32[]{:S(2)}) async-start(), calls=%async_computation.6 | async-start | bytes 5324800
Sparse Core Ops, SparseCore 0:
  28.0 40.8 all-gather.1
  73.7 44.0 reduce-scatter.4
  130.9 245.7 reduce-scatter.6
where the time goes:
time: 387 us; the launch traced here: 383 us
  waiting for transfers between devices  328 us (85%)
  blocking collectives  28 us (7%)
  between operations  13.8 us (4%)
  matrix products  11.6 us (3%)
    unnamed x4, waiting for transfers between devices  243 us
    reduce_scatter x1, waiting for transfers between devices, body(): lax.psum_scatter(lax.dot_general(dh, w_up, (((1,), (1,)), ((), ())), pref...  44.2 us
    all_gather x1, waiting for transfers between devices, body(): lax.all_gather(arrived.reshape(count, width), 'chip', axis=0, tiled=True)  41 us
    all_to_all x1, blocking collectives, body(): lax.all_to_all(picked, 'dp', split_axis=0, concat_axis=0, tiled=True)  18.4 us
    all_to_all x1, blocking collectives, body(): lax.all_to_all(summed.reshape(n_data, depth, width).astype(jnp.bfloat16),...  9.63 us
  transfers between devices with their start and end apart: 3, of which 3 were waited for; matrix products, arithmetic and copies ran while one was open for 1% of the time, Pallas kernels for 0%

commit v1 on v0

v1 whole, which is shorter than its diff:
```python
import jax
import jax.numpy as jnp
from jax import lax
from jax.experimental import pallas as pl
from jax.experimental.pallas import tpu as pltpu
from jax.sharding import PartitionSpec as P

VMEM = pl.BlockSpec(memory_space=pltpu.VMEM)
SMEM = pl.BlockSpec(memory_space=pltpu.SMEM)
F32 = jnp.float32
BF16 = jnp.bfloat16
PARAMS = pltpu.CompilerParams(vmem_limit_bytes=48 * 1024 * 1024)

PIECES = (
    (0, 0), (0, 1),
    (-3, 0), (-3, 1),
    (3, 0), (3, 1),
    (-1, 0), (-1, 1),
    (1, 0), (1, 1),
    (2, 0), (2, 1), (4, 1),
    (-2, 0), (-2, 1), (4, 0),
)


def gelu_slope(value):
    scale = 0.7978845608
    cubic = 0.044715
    inner = jnp.tanh(scale * (value + cubic * value * value * value))
    return 0.5 * (1.0 + inner) + 0.5 * value * (1.0 - inner * inner) * scale * (
        1.0 + 3.0 * cubic * value * value
    )


def pick_kernel(place, slots, tokens, own, other):
    dp, node = place[0], place[1]
    experts = slots.shape[1] // 2
    lane = lax.broadcasted_iota(jnp.int32, slots.shape, 1)
    listed = slots[...]
    token = lax.broadcasted_iota(jnp.int32, (slots.shape[0], tokens.shape[0]), 1)
    for target, out in ((dp, own), (1 - dp, other)):
        expert = target * experts + node // 2
        column = jnp.sum(jnp.where(lane == expert, listed, 0), axis=1, keepdims=True)
        onehot = jnp.where(token == column, 1.0, 0.0).astype(BF16)
        out[...] = jnp.dot(onehot, tokens[...], preferred_element_type=F32).astype(BF16)


def expert_kernel(place, x0, p3, m3, a0, b0, a, b, wt, grad, near_m, near_p, far_m, far_p, keep, dh_out, rows):
    dp, chip = place[0], place[2]
    at = 0
    for ref in (x0, p3, m3, a0, b0, a, b):
        rows[at : at + ref.shape[0], :] = ref[...]
        at += ref.shape[0]
    slots = grad.shape[1]
    row = lax.broadcasted_iota(jnp.int32, (8, slots), 1)
    piece = row // 16
    column = jnp.zeros((8, slots), jnp.int32)
    for number, (offset, half) in enumerate(PIECES):
        first = (lax.rem(chip + offset + 8, 8) * 2 + lax.rem(dp + half, 2)) * 16
        column = jnp.where(piece == number, first, column)
    column = column + row - piece * 16
    given = lax.broadcasted_iota(jnp.int32, (slots, slots), 0)
    order = jnp.where(given == column[:1], 1.0, 0.0).astype(BF16)
    cotangent = jnp.dot(grad[...], order, preferred_element_type=F32)
    pre = lax.dot_general(wt[...], rows[...], (((1,), (1,)), ((), ())), preferred_element_type=F32)
    dh = (cotangent * gelu_slope(pre)).astype(BF16)
    dh_out[...] = dh
    width = wt.shape[1]
    step = 512
    for start in range(0, width, step):
        cols = slice(start, start + step)
        part = lax.dot_general(
            dh, wt[:, cols], (((0,), (0,)), ((), ())), preferred_element_type=F32
        ).astype(BF16)
        keep[:, cols] = part[0:96]
        near_m[:, cols] = part[96:128]
        near_p[:, cols] = part[128:160]
        far_m[0:32, cols] = part[160:192]
        far_p[32:48, cols] = part[192:208]
        far_p[0:32, cols] = part[208:240]
        far_m[32:48, cols] = part[240:256]


def weight_kernel(dh, x0, p3, m3, a0, b0, a, b, out, rows):
    at = 0
    for ref in (x0, p3, m3, a0, b0, a, b):
        rows[at : at + ref.shape[0], :] = ref[...]
        at += ref.shape[0]
    step = 512
    for start in range(0, out.shape[1], step):
        cols = slice(start, start + step)
        out[:, cols] = jnp.dot(dh[...], rows[:, cols], preferred_element_type=F32).astype(BF16)


def middle_kernel(keep, got_p, got_m, to_m, to_p):
    f = lambda value: value.astype(F32)
    to_m[0:16] = (f(keep[32:48]) + f(got_p[0:16]) + f(got_m[32:48])).astype(BF16)
    to_m[16:32] = (f(keep[48:64]) + f(got_p[16:32])).astype(BF16)
    to_p[0:16] = (f(keep[64:80]) + f(got_m[0:16])).astype(BF16)
    to_p[16:32] = (f(keep[80:96]) + f(got_m[16:32]) + f(got_p[32:48])).astype(BF16)


def last_kernel(keep, near_p, near_m, far_p, far_m, own, other):
    for start, out in ((0, own), (16, other)):
        at = slice(start, start + 16)
        out[...] = (
            keep[at].astype(F32)
            + near_p[at].astype(F32)
            + near_m[at].astype(F32)
            + far_p[at].astype(F32)
            + far_m[at].astype(F32)
        ).astype(BF16)


def pack_kernel(own, other, out):
    nodes = out.shape[0]
    wide = own.shape[1] // nodes
    gap = jnp.zeros((own.shape[0], 64 - wide), BF16)
    for node in range(nodes):
        cols = slice(node * wide, (node + 1) * wide)
        out[node] = jnp.concatenate([own[:, cols], gap, other[:, cols], gap], axis=1)


def spread_kernel(place, slots, arrived, out, onehot):
    dp = place[0]
    wide, tokens = out.shape
    depth = slots.shape[0]
    experts = slots.shape[1] // 2
    token = lax.broadcasted_iota(jnp.int32, (depth, tokens), 1)
    total = jnp.zeros((64, tokens), F32)
    for half in range(2):
        swap = lax.rem(dp + half, 2)
        listed = jnp.where(swap == 0, slots[:, :experts], slots[:, experts:])
        for expert in range(experts):
            column = listed[:, expert : expert + 1]
            onehot[expert * depth : (expert + 1) * depth, :] = jnp.where(
                token == column, 1.0, 0.0
            ).astype(BF16)
        for pair in range(2):
            got = arrived[:, pair, :, half * 64 : half * 64 + 64].reshape(experts * depth, 64)
            total += lax.dot_general(
                got, onehot[...], (((0,), (0,)), ((), ())), preferred_element_type=F32
            )
    out[...] = total[:wide]


def shape(rows, columns, dtype=BF16):
    return jax.ShapeDtypeStruct((rows, columns), dtype)


def body(tokens, slot_token, grad_act, w_up):
    tok_grp, width = tokens.shape
    hidden = w_up.shape[1]
    n_nodes = lax.axis_size("node")
    chips = lax.axis_size("chip")
    place = jnp.stack(
        [lax.axis_index("dp"), lax.axis_index("node"), lax.axis_index("chip")]
    ).astype(jnp.int32)
    slots = slot_token[0, 0].T
    depth = slots.shape[0]
    wt = w_up.T
    grad = grad_act.T

    def shift(value, by):
        return lax.ppermute(value, "chip", [(c, (c + by) % chips) for c in range(chips)])

    def swap(value):
        return lax.ppermute(value, "dp", [(0, 1), (1, 0)])

    block = 512
    own, other = pl.pallas_call(
        pick_kernel,
        grid=(width // block,),
        in_specs=[
            SMEM,
            pl.BlockSpec(slots.shape, lambda i: (0, 0)),
            pl.BlockSpec((tok_grp, block), lambda i: (0, i)),
        ],
        out_specs=[pl.BlockSpec((depth, block), lambda i: (0, i))] * 2,
        out_shape=[shape(depth, width)] * 2,
        compiler_params=PARAMS,
    )(place, slots, tokens)
    x0 = jnp.concatenate([own, swap(other)], 0)

    p3, m3 = shift(x0, 3), shift(x0, -3)
    a0, b0 = shift(x0, 1), shift(x0, -1)
    a = shift(jnp.concatenate([m3, p3[16:]], 0), 1)
    b = shift(jnp.concatenate([p3, m3[:16]], 0), -1)
    gathered = (x0, p3, m3, a0, b0, a, b)

    near_m, near_p, far_m, far_p, keep, dh = pl.pallas_call(
        expert_kernel,
        in_specs=[SMEM] + [VMEM] * 9,
        out_specs=[VMEM] * 6,
        out_shape=[
            shape(32, width),
            shape(32, width),
            shape(48, width),
            shape(48, width),
            shape(96, width),
            shape(hidden, 256),
        ],
        scratch_shapes=[pltpu.VMEM((256, width), BF16)],
        compiler_params=PARAMS,
    )(place, *gathered, wt, grad)

    got_p, got_m = shift(far_p, 1), shift(far_m, -1)
    direct_p, direct_m = shift(near_p, 1), shift(near_m, -1)
    grad_wt = pl.pallas_call(
        weight_kernel,
        in_specs=[VMEM] * 8,
        out_specs=VMEM,
        out_shape=shape(hidden, width),
        scratch_shapes=[pltpu.VMEM((256, width), BF16)],
        compiler_params=PARAMS,
        cost_estimate=pl.CostEstimate(flops=2 * 256 * hidden * width, bytes_accessed=5000000, transcendentals=0),
    )(dh, *gathered)
    to_m, to_p = pl.pallas_call(
        middle_kernel,
        in_specs=[VMEM] * 3,
        out_specs=[VMEM] * 2,
        out_shape=[shape(32, width)] * 2,
        compiler_params=PARAMS,
    )(keep, got_p, got_m)
    from_p, from_m = shift(to_p, 3), shift(to_m, -3)
    own_sum, other_sum = pl.pallas_call(
        last_kernel,
        in_specs=[VMEM] * 5,
        out_specs=[VMEM] * 2,
        out_shape=[shape(depth, width)] * 2,
        compiler_params=PARAMS,
    )(keep, direct_p, direct_m, from_p, from_m)
    packed = pl.pallas_call(
        pack_kernel,
        in_specs=[VMEM] * 2,
        out_specs=VMEM,
        out_shape=jax.ShapeDtypeStruct((n_nodes, depth, 128), BF16),
        compiler_params=PARAMS,
    )(own_sum, swap(other_sum))
    arrived = lax.all_to_all(packed, "node", 0, 0, tiled=True)
    grad_xt = pl.pallas_call(
        spread_kernel,
        in_specs=[SMEM, VMEM, VMEM],
        out_specs=VMEM,
        out_shape=shape(width // n_nodes, tok_grp, F32),
        scratch_shapes=[pltpu.VMEM((depth * n_nodes // 2, tok_grp), BF16)],
        compiler_params=PARAMS,
    )(place, slots, arrived.reshape(n_nodes // 2, 2, depth, 128))
    return (grad_wt.T, grad_xt.T)


def solution(mesh):
    placed = (
        P(("dp", "chip"), None),
        P("dp", "chip", None, None),
        P(None, ("dp", "node", "chip")),
        P(None, ("dp", "node", "chip")),
    )
    return jax.shard_map(
        body,
        mesh=mesh,
        in_specs=placed,
        out_specs=(P(None, ("dp", "node", "chip")), P(("dp", "chip"), "node")),
        check_vma=False,
    )
```

time: 387 us -> 129 us (0.33)
  waiting for transfers between devices: 328 us -> 35.6 us
  starting transfers between devices: 0.12 us -> 76.9 us
  blocking collectives: 28 us -> 0 us
  between operations: 13.8 us -> 0.87 us
  matrix products: 11.6 us -> 0 us
  Pallas kernels: 0 us -> 10.3 us
    unnamed x4 -> x0, waiting for transfers between devices: 243 us -> none
    ppermute x0 -> x14, starting transfers between devices: none -> 62.6 us  [the longest x12 39.5 us: shift(): lax.ppermute(value, 'chip', [(c, (c + by) % chips) for c in range(chips)])]
    reduce_scatter x1 -> x0, waiting for transfers between devices: 44.2 us -> none  [body(): lax.psum_scatter(lax.dot_general(dh, w_up, (((1,), (1,)), ((), ())), pref...]
    all_gather x1 -> x0, waiting for transfers between devices: 41 us -> none  [body(): lax.all_gather(arrived.reshape(count, width), 'chip', axis=0, tiled=True)]
    all_to_all x2 -> x0, blocking collectives: 28 us -> none  [the longest x1 18.4 us: body(): lax.all_to_all(picked, 'dp', split_axis=0, concat_axis=0, tiled=True)]
    ppermute x0 -> x14, waiting for transfers between devices: none -> 24.3 us  [the longest x12 22.5 us: shift(): lax.ppermute(value, 'chip', [(c, (c + by) % chips) for c in range(chips)])]
    all_to_all x0 -> x1, starting transfers between devices: none -> 14.3 us  [body(): arrived = lax.all_to_all(packed, 'node', 0, 0, tiled=True)]
    dot_general x5 -> x0, matrix products: 11.6 us -> none  [the longest x1 3.22 us: body(): lax.dot_general(gathered, dh, (((0,), (0,)), ((), ())), preferred_element...]
  transfers between devices with their start and end apart: 3 -> 15, of which waited for: 3 -> 8; matrix products, arithmetic and copies ran while one was open for 1% -> 0% of each run, Pallas kernels for 0% -> 1%
where the time goes in v1:
time: 129 us; the launch traced here: 126 us
  starting transfers between devices  76.9 us (60%)
  waiting for transfers between devices  35.6 us (28%)
  Pallas kernels  10.3 us (8%)
  local copies, waits for them, and re-layouts  2.48 us (2%)
    ppermute x12, starting transfers between devices, shift(): lax.ppermute(value, 'chip', [(c, (c + by) % chips) for c in range(chips)])  39.5 us
    ppermute x2, starting transfers between devices, swap(): return lax.ppermute(value, 'dp', [(0, 1), (1, 0)])  23.1 us
    ppermute x12, waiting for transfers between devices, shift(): lax.ppermute(value, 'chip', [(c, (c + by) % chips) for c in range(chips)])  22.5 us
    all_to_all x1, starting transfers between devices, body(): arrived = lax.all_to_all(packed, 'node', 0, 0, tiled=True)  14.3 us
    all_to_all x1, waiting for transfers between devices, body(): arrived = lax.all_to_all(packed, 'node', 0, 0, tiled=True)  11.3 us
    pallas_call x1, Pallas kernels, body(): pl.pallas_call(expert_kernel, in_specs=[SMEM] + [VMEM] * 9, out_specs=[VM...  2.93 us
  transfers between devices with their start and end apart: 15, of which 8 were waited for; matrix products, arithmetic and copies ran while one was open for 0% of the time, Pallas kernels for 1%

profile of v1, /device:TPU:1, one launch (start us, length us, event | category | flops | bytes accessed | tf_op | source)
XLA Modules:
  0.0 126.2 jit_solution(867964395619524504)
XLA Ops:
  0.7 1.7 %copy-done = bf16[512,2560]{1,0:T(8,128)(2,1)S(1)} copy-done((bf16[512,2560]{1,0:T(8,128)(2,1)S(1)}, bf16[512,2560]{1,0:T(8,128)(2,1)}, u32[]{:S(2)}) %copy-start) | copy-done | bytes 2621464
  2.5 0.7 copy-done.3
  3.2 2.3 %shard_map.59 = (bf16[16,2560]{1,0:T(8,128)(2,1)S(1)}, bf16[16,2560]{1,0:T(8,128)(2,1)S(1)}) custom-call(s32[3]{0:T(128)S(1)} %pad_add_fusion.place, s32[16,64]{1,0:T(8,128)S(1)} %bitcast.14, bf16[512,2560]{1,0:T(8,128)(2,1)S(1)} %copy-done), custom_call_target="tpu_custom_call" | custom-call | tf_op jit(solution)/shard_map/pallas_call | solution.py:170
  5.5 16.1 %collective-permute-start = (bf16[16,2560]{1,0:T(8,128)(2,1)S(1)}, bf16[16,2560]{1,0:T(8,128)(2,1)S(1)}, u32[]{:S(2)}, u32[]{:S(2)}) collective-permute-start(bf16[16,2560]{1,0:T(8,128)(2,1)S(1)} %get-tuple-element.15), channel_id=1, source_target_pairs={{0,512},{512,0},{1,513},{513,1},{2,514},{514,2},{3,515},{515,3},{4... | collective-permute-start | bytes 245768 | tf_op jit(solution)/shard_map/ppermute | solution.py:167
  21.6 0.9 collective-permute-done
  22.4 2.5 %collective-permute-start.2 = (bf16[32,2560]{1,0:T(8,128)(2,1)S(1)}, bf16[32,2560]{1,0:T(8,128)(2,1)S(1)}, u32[]{:S(2)}, u32[]{:S(2)}) collective-permute-start(bf16[32,2560]{1,0:T(8,128)(2,1)S(1)} %constant_dynamic-update-slice_fusion.x0), channel_id=1, source_target_pairs={{0,5},{1,6},{2,7},{3,0},{4,1},{5,2},{6,3},{7,4},{8,13},{9,14},{10,... | collective-permute-start | bytes 491528 | tf_op jit(solution)/shard_map/ppermute | solution.py:164
  25.0 4.5 %collective-permute-start.1 = (bf16[32,2560]{1,0:T(8,128)(2,1)S(1)}, bf16[32,2560]{1,0:T(8,128)(2,1)S(1)}, u32[]{:S(2)}, u32[]{:S(2)}) collective-permute-start(bf16[32,2560]{1,0:T(8,128)(2,1)S(1)} %constant_dynamic-update-slice_fusion.x0), channel_id=1, source_target_pairs={{0,3},{1,4},{2,5},{3,6},{4,7},{5,0},{6,1},{7,2},{8,11},{9,12},{10,... | collective-permute-start | bytes 491528 | tf_op jit(solution)/shard_map/ppermute | solution.py:164
  29.5 5.9 %collective-permute-done.2.m3 = bf16[32,2560]{1,0:T(8,128)(2,1)S(1)} collective-permute-done((bf16[32,2560]{1,0:T(8,128)(2,1)S(1)}, bf16[32,2560]{1,0:T(8,128)(2,1)S(1)}, u32[]{:S(2)}, u32[]{:S(2)}) %collective-permute-start.2) | collective-permute-done | bytes 163872 | tf_op jit(solution)/shard_map/ppermute | solution.py:164
  35.4 7.3 %collective-permute-done.1.p3 = bf16[32,2560]{1,0:T(8,128)(2,1)S(1)} collective-permute-done((bf16[32,2560]{1,0:T(8,128)(2,1)S(1)}, bf16[32,2560]{1,0:T(8,128)(2,1)S(1)}, u32[]{:S(2)}, u32[]{:S(2)}) %collective-permute-start.1) | collective-permute-done | bytes 163872 | tf_op jit(solution)/shard_map/ppermute | solution.py:164
  42.7 1.9 %collective-permute-start.6 = (bf16[48,2560]{1,0:T(8,128)(2,1)S(1)}, bf16[48,2560]{1,0:T(8,128)(2,1)S(1)}, u32[]{:S(2)}, u32[]{:S(2)}) collective-permute-start(bf16[48,2560]{1,0:T(8,128)(2,1)S(1)} %pad_maximum_fusion.1), channel_id=1, source_target_pairs={{0,7},{1,0},{2,1},{3,2},{4,3},{5,4},{6,5},{7,6},{8,15},{9,8},{10,9... | collective-permute-start | bytes 737288 | tf_op jit(solution)/shard_map/ppermute | solution.py:164
  44.7 3.4 %collective-permute-start.5 = (bf16[48,2560]{1,0:T(8,128)(2,1)S(1)}, bf16[48,2560]{1,0:T(8,128)(2,1)S(1)}, u32[]{:S(2)}, u32[]{:S(2)}) collective-permute-start(bf16[48,2560]{1,0:T(8,128)(2,1)S(1)} %pad_maximum_fusion), channel_id=1, source_target_pairs={{0,1},{1,2},{2,3},{3,4},{4,5},{5,6},{6,7},{7,0},{8,9},{9,10},{10,1... | collective-permute-start | bytes 737288 | tf_op jit(solution)/shard_map/ppermute | solution.py:164
  48.0 1.9 %collective-permute-start.3 = (bf16[32,2560]{1,0:T(8,128)(2,1)S(1)}, bf16[32,2560]{1,0:T(8,128)(2,1)S(1)}, u32[]{:S(2)}, u32[]{:S(2)}) collective-permute-start(bf16[32,2560]{1,0:T(8,128)(2,1)S(1)} %constant_dynamic-update-slice_fusion.x0), channel_id=1, source_target_pairs={{0,1},{1,2},{2,3},{3,4},{4,5},{5,6},{6,7},{7,0},{8,9},{9,10},{10,1... | collective-permute-start | bytes 491528 | tf_op jit(solution)/shard_map/ppermute | solution.py:164
  50.0 4.6 %collective-permute-start.4 = (bf16[32,2560]{1,0:T(8,128)(2,1)S(1)}, bf16[32,2560]{1,0:T(8,128)(2,1)S(1)}, u32[]{:S(2)}, u32[]{:S(2)}) collective-permute-start(bf16[32,2560]{1,0:T(8,128)(2,1)S(1)} %constant_dynamic-update-slice_fusion.x0), channel_id=1, source_target_pairs={{0,7},{1,0},{2,1},{3,2},{4,3},{5,4},{6,5},{7,6},{8,15},{9,8},{10,9... | collective-permute-start | bytes 491528 | tf_op jit(solution)/shard_map/ppermute | solution.py:164
  54.6 3.3 %collective-permute-done.3.a0 = bf16[32,2560]{1,0:T(8,128)(2,1)S(1)} collective-permute-done((bf16[32,2560]{1,0:T(8,128)(2,1)S(1)}, bf16[32,2560]{1,0:T(8,128)(2,1)S(1)}, u32[]{:S(2)}, u32[]{:S(2)}) %collective-permute-start.3) | collective-permute-done | bytes 163872 | tf_op jit(solution)/shard_map/ppermute | solution.py:164
  57.9 2.9 %shard_map.60 = (bf16[32,2560]{1,0:T(8,128)(2,1)S(1)}, bf16[32,2560]{1,0:T(8,128)(2,1)S(1)}, bf16[48,2560]{1,0:T(8,128)(2,1)S(1)}, bf16[48,2560]{1,0:T(8,128)(2,...) custom-call(s32[3]{0:T(128)S(1)} %pad_add_fusion.place, ...), custom_call_target="tpu_custom_call" | custom-call | tf_op jit(solution)/shard_map/pallas_call | solution.py:190
  60.8 4.0 %collective-permute-start.10 = (bf16[48,2560]{1,0:T(8,128)(2,1)S(1)}, bf16[48,2560]{1,0:T(8,128)(2,1)S(1)}, u32[]{:S(2)}, u32[]{:S(2)}) collective-permute-start(bf16[48,2560]{1,0:T(8,128)(2,1)S(1)} %get-tuple-element.21), channel_id=1, source_target_pairs={{0,7},{1,0},{2,1},{3,2},{4,3},{5,4},{6,5},{7,6},{8,15},{9,8},{10,9... | collective-permute-start | bytes 737288 | tf_op jit(solution)/shard_map/ppermute | solution.py:164
  64.8 1.9 %collective-permute-start.9 = (bf16[48,2560]{1,0:T(8,128)(2,1)S(1)}, bf16[48,2560]{1,0:T(8,128)(2,1)S(1)}, u32[]{:S(2)}, u32[]{:S(2)}) collective-permute-start(bf16[48,2560]{1,0:T(8,128)(2,1)S(1)} %get-tuple-element.20), channel_id=1, source_target_pairs={{0,1},{1,2},{2,3},{3,4},{4,5},{5,6},{6,7},{7,0},{8,9},{9,10},{10,1... | collective-permute-start | bytes 737288 | tf_op jit(solution)/shard_map/ppermute | solution.py:164
  66.7 1.9 %collective-permute-start.7 = (bf16[32,2560]{1,0:T(8,128)(2,1)S(1)}, bf16[32,2560]{1,0:T(8,128)(2,1)S(1)}, u32[]{:S(2)}, u32[]{:S(2)}) collective-permute-start(bf16[32,2560]{1,0:T(8,128)(2,1)S(1)} %get-tuple-element.18), channel_id=1, source_target_pairs={{0,1},{1,2},{2,3},{3,4},{4,5},{5,6},{6,7},{7,0},{8,9},{9,10},{10,1... | collective-permute-start | bytes 491528 | tf_op jit(solution)/shard_map/ppermute | solution.py:164
  68.6 4.6 %collective-permute-start.8 = (bf16[32,2560]{1,0:T(8,128)(2,1)S(1)}, bf16[32,2560]{1,0:T(8,128)(2,1)S(1)}, u32[]{:S(2)}, u32[]{:S(2)}) collective-permute-start(bf16[32,2560]{1,0:T(8,128)(2,1)S(1)} %get-tuple-element.19), channel_id=1, source_target_pairs={{0,7},{1,0},{2,1},{3,2},{4,3},{5,4},{6,5},{7,6},{8,15},{9,8},{10,9... | collective-permute-start | bytes 491528 | tf_op jit(solution)/shard_map/ppermute | solution.py:164
  73.2 0.1 shard_map.62
  73.4 2.0 %collective-permute-start.11 = (bf16[32,2560]{1,0:T(8,128)(2,1)S(1)}, bf16[32,2560]{1,0:T(8,128)(2,1)S(1)}, u32[]{:S(2)}, u32[]{:S(2)}) collective-permute-start(bf16[32,2560]{1,0:T(8,128)(2,1)S(1)} %get-tuple-element.22), channel_id=1, source_target_pairs={{0,3},{1,4},{2,5},{3,6},{4,7},{5,0},{6,1},{7,2},{8,11},{9,12},{10,... | collective-permute-start | bytes 491528 | tf_op jit(solution)/shard_map/ppermute | solution.py:164
  75.4 6.3 %collective-permute-start.12 = (bf16[32,2560]{1,0:T(8,128)(2,1)S(1)}, bf16[32,2560]{1,0:T(8,128)(2,1)S(1)}, u32[]{:S(2)}, u32[]{:S(2)}) collective-permute-start(bf16[32,2560]{1,0:T(8,128)(2,1)S(1)} %get-tuple-element.23), channel_id=1, source_target_pairs={{0,5},{1,6},{2,7},{3,0},{4,1},{5,2},{6,3},{7,4},{8,13},{9,14},{10,... | collective-permute-start | bytes 491528 | tf_op jit(solution)/shard_map/ppermute | solution.py:164
  81.7 4.7 %collective-permute-done.11.far_p = bf16[32,2560]{1,0:T(8,128)(2,1)S(1)} collective-permute-done((bf16[32,2560]{1,0:T(8,128)(2,1)S(1)}, bf16[32,2560]{1,0:T(8,128)(2,1)S(1)}, u32[]{:S(2)}, u32[]{:S(2)}) %collective-permute-start.11) | collective-permute-done | bytes 163872 | tf_op jit(solution)/shard_map/ppermute | solution.py:164
  86.4 1.3 %collective-permute-done.12.far_m = bf16[32,2560]{1,0:T(8,128)(2,1)S(1)} collective-permute-done((bf16[32,2560]{1,0:T(8,128)(2,1)S(1)}, bf16[32,2560]{1,0:T(8,128)(2,1)S(1)}, u32[]{:S(2)}, u32[]{:S(2)}) %collective-permute-start.12) | collective-permute-done | bytes 163872 | tf_op jit(solution)/shard_map/ppermute | solution.py:164
  87.7 0.1 shard_map.63
  87.8 7.0 %collective-permute-start.13 = (bf16[16,2560]{1,0:T(8,128)(2,1)S(1)}, bf16[16,2560]{1,0:T(8,128)(2,1)S(1)}, u32[]{:S(2)}, u32[]{:S(2)}) collective-permute-start(bf16[16,2560]{1,0:T(8,128)(2,1)S(1)} %get-tuple-element.25), channel_id=1, source_target_pairs={{0,512},{512,0},{1,513},{513,1},{2,514},{514,2},{3,515},{515,3},{4... | collective-permute-start | bytes 245768 | tf_op jit(solution)/shard_map/ppermute | solution.py:167
  94.8 0.9 collective-permute-done.13.other
  95.7 0.9 shard_map.64
  96.7 14.3 %all-to-all-start = ((bf16[64,16,128]{2,1,0:T(8,128)(2,1)}), bf16[64,16,128]{2,1,0:T(8,128)(2,1)S(1)}, u32[]{:S(2)}, u32[]{:S(2)}) async-start(bf16[64,16,128]{2,1,0:T(8,128)(2,1)} %shard_map.64), calls=%async_computation | async-start | bytes 524288 | tf_op jit(solution)/shard_map/all_to_all | solution.py:239
  111.0 1.8 %shard_map.61 = bf16[320,2560]{1,0:T(8,128)(2,1)} custom-call(bf16[320,256]{1,0:T(8,128)(2,1)S(1)} %get-tuple-element.16.dh, bf16[32,2560]{1,0:T(8,128)(2,1)S(1)} %constant_dynamic-update-slice_fusion.x0, bf16[32,2560]{1,0:T(8,128)(2,1)S(1)} %collective-permute-done.1.p3, bf16[32,2560]{1,0:T(8,128)(2,1)S(1)} %collective-permute-done.2.m3, ...), custom_call_target="tpu_custom_call" | custom-call | flops 419430400 | bytes 5000000 | tf_op jit(solution)/shard_map/pallas_call | solution.py:208
  112.8 11.3 %all-to-all-done = bf16[64,16,128]{2,1,0:T(8,128)(2,1)S(1)} async-done(((bf16[64,16,128]{2,1,0:T(8,128)(2,1)}), bf16[64,16,128]{2,1,0:T(8,128)(2,1)S(1)}, u32[]{:S(2)}, u32[]{:S(2)}) %all-to-all-start) | async-done | bytes 262176 | tf_op jit(solution)/shard_map/all_to_all | solution.py:239
  124.1 2.1 %shard_map.65 = f32[40,512]{1,0:T(8,128)} custom-call(s32[3]{0:T(128)S(1)} %pad_add_fusion.place, s32[16,64]{1,0:T(8,128)S(1)} %bitcast.15, bf16[32,2,16,128]{3,2,1,0:T(8,128)(2,1)S(1)} %bitcast.12), custom_call_target="tpu_custom_call" | custom-call | tf_op jit(solution)/shard_map/pallas_call | solution.py:240
  (22 shorter events, 0.2 us)
Async XLA Ops:
  0.7 1.7 %copy-start = (bf16[512,2560]{1,0:T(8,128)(2,1)S(1)}, bf16[512,2560]{1,0:T(8,128)(2,1)}, u32[]{:S(2)}) copy-start(bf16[512,2560]{1,0:T(8,128)(2,1)} %tokens.1) | copy-start | bytes 7864324
  2.5 0.7 copy-start.3
  3.2 54.7 %copy-start.1 = (bf16[2560,320]{0,1:T(8,128)(2,1)S(1)}, bf16[2560,320]{0,1:T(8,128)(2,1)}, u32[]{:S(2)}) copy-start(bf16[2560,320]{0,1:T(8,128)(2,1)} %param.7) | copy-start | bytes 4915204
  3.2 54.7 %copy-start.2 = (bf16[256,320]{0,1:T(8,128)(2,1)S(1)}, bf16[256,320]{0,1:T(8,128)(2,1)}, u32[]{:S(2)}) copy-start(bf16[256,320]{0,1:T(8,128)(2,1)} %param.6) | copy-start | bytes 491524
  5.5 17.0 %collective-permute-start = (bf16[16,2560]{1,0:T(8,128)(2,1)S(1)}, bf16[16,2560]{1,0:T(8,128)(2,1)S(1)}, u32[]{:S(2)}, u32[]{:S(2)}) collective-permute-start(bf16[16,2560]{1,0:T(8,128)(2,1)S(1)} %get-tuple-element.15), channel_id=1, source_target_pairs={{0,512},{512,0},{1,513},{513,1},{2,514},{514,2},{3,515},{515,3},{4... | collective-permute-start | bytes 245768 | tf_op jit(solution)/shard_map/ppermute | solution.py:167
  22.4 12.9 %collective-permute-start.2 = (bf16[32,2560]{1,0:T(8,128)(2,1)S(1)}, bf16[32,2560]{1,0:T(8,128)(2,1)S(1)}, u32[]{:S(2)}, u32[]{:S(2)}) collective-permute-start(bf16[32,2560]{1,0:T(8,128)(2,1)S(1)} %constant_dynamic-update-slice_fusion.x0), channel_id=1, source_target_pairs={{0,5},{1,6},{2,7},{3,0},{4,1},{5,2},{6,3},{7,4},{8,13},{9,14},{10,... | collective-permute-start | bytes 491528 | tf_op jit(solution)/shard_map/ppermute | solution.py:164
  25.0 17.7 %collective-permute-start.1 = (bf16[32,2560]{1,0:T(8,128)(2,1)S(1)}, bf16[32,2560]{1,0:T(8,128)(2,1)S(1)}, u32[]{:S(2)}, u32[]{:S(2)}) collective-permute-start(bf16[32,2560]{1,0:T(8,128)(2,1)S(1)} %constant_dynamic-update-slice_fusion.x0), channel_id=1, source_target_pairs={{0,3},{1,4},{2,5},{3,6},{4,7},{5,0},{6,1},{7,2},{8,11},{9,12},{10,... | collective-permute-start | bytes 491528 | tf_op jit(solution)/shard_map/ppermute | solution.py:164
  42.7 15.1 %collective-permute-start.6 = (bf16[48,2560]{1,0:T(8,128)(2,1)S(1)}, bf16[48,2560]{1,0:T(8,128)(2,1)S(1)}, u32[]{:S(2)}, u32[]{:S(2)}) collective-permute-start(bf16[48,2560]{1,0:T(8,128)(2,1)S(1)} %pad_maximum_fusion.1), channel_id=1, source_target_pairs={{0,7},{1,0},{2,1},{3,2},{4,3},{5,4},{6,5},{7,6},{8,15},{9,8},{10,9... | collective-permute-start | bytes 737288 | tf_op jit(solution)/shard_map/ppermute | solution.py:164
  44.7 13.2 %collective-permute-start.5 = (bf16[48,2560]{1,0:T(8,128)(2,1)S(1)}, bf16[48,2560]{1,0:T(8,128)(2,1)S(1)}, u32[]{:S(2)}, u32[]{:S(2)}) collective-permute-start(bf16[48,2560]{1,0:T(8,128)(2,1)S(1)} %pad_maximum_fusion), channel_id=1, source_target_pairs={{0,1},{1,2},{2,3},{3,4},{4,5},{5,6},{6,7},{7,0},{8,9},{9,10},{10,1... | collective-permute-start | bytes 737288 | tf_op jit(solution)/shard_map/ppermute | solution.py:164
  48.0 9.8 %collective-permute-start.3 = (bf16[32,2560]{1,0:T(8,128)(2,1)S(1)}, bf16[32,2560]{1,0:T(8,128)(2,1)S(1)}, u32[]{:S(2)}, u32[]{:S(2)}) collective-permute-start(bf16[32,2560]{1,0:T(8,128)(2,1)S(1)} %constant_dynamic-update-slice_fusion.x0), channel_id=1, source_target_pairs={{0,1},{1,2},{2,3},{3,4},{4,5},{5,6},{6,7},{7,0},{8,9},{9,10},{10,1... | collective-permute-start | bytes 491528 | tf_op jit(solution)/shard_map/ppermute | solution.py:164
  50.0 7.9 %collective-permute-start.4 = (bf16[32,2560]{1,0:T(8,128)(2,1)S(1)}, bf16[32,2560]{1,0:T(8,128)(2,1)S(1)}, u32[]{:S(2)}, u32[]{:S(2)}) collective-permute-start(bf16[32,2560]{1,0:T(8,128)(2,1)S(1)} %constant_dynamic-update-slice_fusion.x0), channel_id=1, source_target_pairs={{0,7},{1,0},{2,1},{3,2},{4,3},{5,4},{6,5},{7,6},{8,15},{9,8},{10,9... | collective-permute-start | bytes 491528 | tf_op jit(solution)/shard_map/ppermute | solution.py:164
  60.8 12.4 %collective-permute-start.10 = (bf16[48,2560]{1,0:T(8,128)(2,1)S(1)}, bf16[48,2560]{1,0:T(8,128)(2,1)S(1)}, u32[]{:S(2)}, u32[]{:S(2)}) collective-permute-start(bf16[48,2560]{1,0:T(8,128)(2,1)S(1)} %get-tuple-element.21), channel_id=1, source_target_pairs={{0,7},{1,0},{2,1},{3,2},{4,3},{5,4},{6,5},{7,6},{8,15},{9,8},{10,9... | collective-permute-start | bytes 737288 | tf_op jit(solution)/shard_map/ppermute | solution.py:164
  64.8 8.5 %collective-permute-start.9 = (bf16[48,2560]{1,0:T(8,128)(2,1)S(1)}, bf16[48,2560]{1,0:T(8,128)(2,1)S(1)}, u32[]{:S(2)}, u32[]{:S(2)}) collective-permute-start(bf16[48,2560]{1,0:T(8,128)(2,1)S(1)} %get-tuple-element.20), channel_id=1, source_target_pairs={{0,1},{1,2},{2,3},{3,4},{4,5},{5,6},{6,7},{7,0},{8,9},{9,10},{10,1... | collective-permute-start | bytes 737288 | tf_op jit(solution)/shard_map/ppermute | solution.py:164
  66.7 14.9 %collective-permute-start.7 = (bf16[32,2560]{1,0:T(8,128)(2,1)S(1)}, bf16[32,2560]{1,0:T(8,128)(2,1)S(1)}, u32[]{:S(2)}, u32[]{:S(2)}) collective-permute-start(bf16[32,2560]{1,0:T(8,128)(2,1)S(1)} %get-tuple-element.18), channel_id=1, source_target_pairs={{0,1},{1,2},{2,3},{3,4},{4,5},{5,6},{6,7},{7,0},{8,9},{9,10},{10,1... | collective-permute-start | bytes 491528 | tf_op jit(solution)/shard_map/ppermute | solution.py:164
  68.6 13.0 %collective-permute-start.8 = (bf16[32,2560]{1,0:T(8,128)(2,1)S(1)}, bf16[32,2560]{1,0:T(8,128)(2,1)S(1)}, u32[]{:S(2)}, u32[]{:S(2)}) collective-permute-start(bf16[32,2560]{1,0:T(8,128)(2,1)S(1)} %get-tuple-element.19), channel_id=1, source_target_pairs={{0,7},{1,0},{2,1},{3,2},{4,3},{5,4},{6,5},{7,6},{8,15},{9,8},{10,9... | collective-permute-start | bytes 491528 | tf_op jit(solution)/shard_map/ppermute | solution.py:164
  73.4 13.1 %collective-permute-start.11 = (bf16[32,2560]{1,0:T(8,128)(2,1)S(1)}, bf16[32,2560]{1,0:T(8,128)(2,1)S(1)}, u32[]{:S(2)}, u32[]{:S(2)}) collective-permute-start(bf16[32,2560]{1,0:T(8,128)(2,1)S(1)} %get-tuple-element.22), channel_id=1, source_target_pairs={{0,3},{1,4},{2,5},{3,6},{4,7},{5,0},{6,1},{7,2},{8,11},{9,12},{10,... | collective-permute-start | bytes 491528 | tf_op jit(solution)/shard_map/ppermute | solution.py:164
  75.4 12.4 %collective-permute-start.12 = (bf16[32,2560]{1,0:T(8,128)(2,1)S(1)}, bf16[32,2560]{1,0:T(8,128)(2,1)S(1)}, u32[]{:S(2)}, u32[]{:S(2)}) collective-permute-start(bf16[32,2560]{1,0:T(8,128)(2,1)S(1)} %get-tuple-element.23), channel_id=1, source_target_pairs={{0,5},{1,6},{2,7},{3,0},{4,1},{5,2},{6,3},{7,4},{8,13},{9,14},{10,... | collective-permute-start | bytes 491528 | tf_op jit(solution)/shard_map/ppermute | solution.py:164
  87.8 7.9 %collective-permute-start.13 = (bf16[16,2560]{1,0:T(8,128)(2,1)S(1)}, bf16[16,2560]{1,0:T(8,128)(2,1)S(1)}, u32[]{:S(2)}, u32[]{:S(2)}) collective-permute-start(bf16[16,2560]{1,0:T(8,128)(2,1)S(1)} %get-tuple-element.25), channel_id=1, source_target_pairs={{0,512},{512,0},{1,513},{513,1},{2,514},{514,2},{3,515},{515,3},{4... | collective-permute-start | bytes 245768 | tf_op jit(solution)/shard_map/ppermute | solution.py:167
  96.7 27.4 %all-to-all-start = ((bf16[64,16,128]{2,1,0:T(8,128)(2,1)}), bf16[64,16,128]{2,1,0:T(8,128)(2,1)S(1)}, u32[]{:S(2)}, u32[]{:S(2)}) async-start(bf16[64,16,128]{2,1,0:T(8,128)(2,1)} %shard_map.64), calls=%async_computation | async-start | bytes 524288 | tf_op jit(solution)/shard_map/all_to_all | solution.py:239
  111.0 13.1 %copy-start.4 = (s32[1,1,64,16]{2,3,1,0:T(8,128)S(1)}, s32[1,1,64,16]{2,3,1,0:T(8,128)}, u32[]{:S(2)}) copy-start(s32[1,1,64,16]{2,3,1,0:T(8,128)} %param.5) | copy-start | bytes 12292

commit v2 on v1

v2 whole, which is shorter than its diff:
```python
import functools

import jax
import jax.numpy as jnp
from jax import lax
from jax.experimental import pallas as pl
from jax.experimental.pallas import tpu as pltpu
from jax.sharding import PartitionSpec as P

VMEM = pl.BlockSpec(memory_space=pltpu.VMEM)
HBM = pl.BlockSpec(memory_space=pltpu.HBM)
F32 = jnp.float32
BF16 = jnp.bfloat16
WAIT = pl.CostEstimate(flops=20_000_000_000, bytes_accessed=0, transcendentals=0)
PARAMS = pltpu.CompilerParams(vmem_limit_bytes=24 * 1024 * 1024)

HELD = (0, -2, 2, 4)
SENT = (-1, -3, 1, 3)


def gelu_slope(value):
    scale = 0.7978845608
    cubic = 0.044715
    inner = jnp.tanh(scale * (value + cubic * value * value * value))
    return 0.5 * (1.0 + inner) + 0.5 * value * (1.0 - inner * inner) * scale * (
        1.0 + 3.0 * cubic * value * value
    )


def pick_kernel(slots_from, tokens_from, own, other, slots, tokens, done):
    dp, node = lax.axis_index("dp"), lax.axis_index("node")
    depth = slots.shape[0]
    experts = slots.shape[1] // 2
    step = 512
    lists = pltpu.make_async_copy(slots_from, slots, done.at[0])
    lists.start()
    copies = []
    for number, start in enumerate(range(0, tokens.shape[1], step)):
        cols = pl.ds(start, step)
        copies.append(
            pltpu.make_async_copy(tokens_from.at[:, cols], tokens.at[:, cols], done.at[number + 1])
        )
        copies[-1].start()
    lists.wait()
    lane = lax.broadcasted_iota(jnp.int32, slots.shape, 1)
    listed = slots[...]
    token = lax.broadcasted_iota(jnp.int32, (2 * depth, tokens.shape[0]), 1)
    columns = [
        jnp.sum(jnp.where(lane == target * experts + node // 2, listed, 0), axis=1, keepdims=True)
        for target in (dp, 1 - dp)
    ]
    onehot = jnp.where(token == jnp.concatenate(columns, axis=0), 1.0, 0.0).astype(BF16)
    for number, start in enumerate(range(0, tokens.shape[1], step)):
        cols = slice(start, start + step)
        copies[number].wait()
        rows = jnp.dot(onehot, tokens[:, cols], preferred_element_type=F32).astype(BF16)
        own[:, cols] = rows[:depth]
        other[:, cols] = rows[depth:]


def prepare_kernel(slots, grad, held, sent, onehot):
    dp, chip = lax.axis_index("dp"), lax.axis_index("chip")
    total = grad.shape[1]
    for blocks, out in ((HELD, held), (SENT, sent)):
        count = 32 * len(blocks)
        row = lax.broadcasted_iota(jnp.int32, (8, count), 1)
        block = row // 32
        half = row // 16 - 2 * block
        column = row - 16 * (row // 16) + 16 * jnp.where(half == 0, dp, 1 - dp)
        for number, offset in enumerate(blocks):
            first = lax.rem(chip + offset + 8, 8) * 32
            column = jnp.where(block == number, column + first, column)
        given = lax.broadcasted_iota(jnp.int32, (total, count), 0)
        order = jnp.where(given == column[:1], 1.0, 0.0).astype(BF16)
        out[...] = jnp.dot(grad[...], order, preferred_element_type=F32).astype(BF16)
    depth = slots.shape[0]
    experts = slots.shape[1] // 2
    tokens = onehot.shape[2]
    token = lax.broadcasted_iota(jnp.int32, (depth, tokens), 1)
    for half in range(2):
        swap = lax.rem(dp + half, 2)
        listed = jnp.where(swap == 0, slots[:, :experts], slots[:, experts:])
        for expert in range(experts):
            column = listed[:, expert : expert + 1]
            onehot[half, expert * depth : (expert + 1) * depth, :] = jnp.where(
                token == column, 1.0, 0.0
            ).astype(BF16)


def fill(rows, *pieces):
    at = 0
    for ref in pieces:
        rows[at : at + ref.shape[0], :] = ref[...]
        at += ref.shape[0]


def expert_kernel(pieces, *refs):
    given, wt, grad = refs[:pieces], refs[pieces], refs[pieces + 1]
    parts, dh_out, rows = refs[pieces + 2 : -2], refs[-2], refs[-1]
    fill(rows, *given)
    pre = lax.dot_general(wt[...], rows[...], (((1,), (1,)), ((), ())), preferred_element_type=F32)
    dh = (grad[...].astype(F32) * gelu_slope(pre)).astype(BF16)
    dh_out[...] = dh
    step = 512
    for start in range(0, wt.shape[1], step):
        cols = slice(start, start + step)
        part = lax.dot_general(
            dh, wt[:, cols], (((0,), (0,)), ((), ())), preferred_element_type=F32
        ).astype(BF16)
        at = 0
        for out in parts:
            out[:, cols] = part[at : at + out.shape[0]]
            at += out.shape[0]


def join_kernel(x0, p2, m2, to_p, to_m):
    fill(to_p, x0, p2)
    fill(to_m, x0, m2)


def weight_kernel(dh_held, dh_sent, x0, p2, m2, p1, m1, far, out, rows, dh):
    fill(rows, x0, p2, m2, far, p1, m1)
    at = 0
    for ref in (dh_held, dh_sent):
        dh[:, at : at + ref.shape[1]] = ref[...]
        at += ref.shape[1]
    step = 512
    for start in range(0, out.shape[1], step):
        cols = slice(start, start + step)
        out[:, cols] = jnp.dot(dh[...], rows[:, cols], preferred_element_type=F32).astype(BF16)


def middle_kernel(keep, got_p, got_m, to_p, to_m):
    f = lambda value: value.astype(F32)
    to_m[...] = (f(keep[32:64]) + f(got_m[32:64])).astype(BF16)
    to_p[...] = (f(keep[64:96]) + f(got_p[32:64])).astype(BF16)


def across_kernel(keep, across, out):
    out[...] = keep[0:32].astype(F32) + across[...].astype(F32)


def last_kernel(near, got_p, got_m, from_p, from_m, own, other):
    for start, out in ((0, own), (16, other)):
        at = slice(start, start + 16)
        total = near[at]
        for ref in (got_p, got_m, from_p, from_m):
            total = total + ref[at].astype(F32)
        out[...] = total.astype(BF16)


def pack_kernel(own, other, out):
    nodes = out.shape[0]
    wide = own.shape[1] // nodes
    gap = jnp.zeros((own.shape[0], 64 - wide), BF16)
    for node in range(nodes):
        cols = slice(node * wide, (node + 1) * wide)
        out[node] = jnp.concatenate([own[:, cols], gap, other[:, cols], gap], axis=1)


def spread_kernel(onehot, arrived, out):
    wide, tokens = out.shape
    total = jnp.zeros((64, tokens), F32)
    for half in range(2):
        for pair in range(2):
            got = arrived[:, pair, :, half * 64 : half * 64 + 64].reshape(onehot.shape[1], 64)
            total += lax.dot_general(
                got, onehot[half], (((0,), (0,)), ((), ())), preferred_element_type=F32
            )
    out[...] = total[:wide]


def shape(rows, columns, dtype=BF16):
    return jax.ShapeDtypeStruct((rows, columns), dtype)


def body(tokens, slot_token, grad_act, w_up):
    tok_grp, width = tokens.shape
    hidden = w_up.shape[1]
    n_nodes = lax.axis_size("node")
    chips = lax.axis_size("chip")
    slots = slot_token[0, 0].T
    depth = slots.shape[0]
    wt = w_up.T
    grad = grad_act.T

    def shift(value, by):
        return lax.ppermute(value, "chip", [(c, (c + by) % chips) for c in range(chips)])

    def swap(value):
        return lax.ppermute(value, "dp", [(0, 1), (1, 0)])

    own, other = pl.pallas_call(
        pick_kernel,
        in_specs=[HBM] * 2,
        out_specs=[VMEM] * 2,
        out_shape=[shape(depth, width)] * 2,
        scratch_shapes=[
            pltpu.VMEM(slots.shape, jnp.int32),
            pltpu.VMEM(tokens.shape, BF16),
            pltpu.SemaphoreType.DMA((width // 512 + 1,)),
        ],
        compiler_params=pltpu.CompilerParams(vmem_limit_bytes=62 * 1024 * 1024),
    )(slots, tokens)
    x0 = jnp.concatenate([own, swap(other)], 0)

    def expert(rows, cotangent, sizes, cost=None):
        count = cotangent.shape[1]
        return pl.pallas_call(
            functools.partial(expert_kernel, len(rows)),
            in_specs=[VMEM] * (len(rows) + 2),
            out_specs=[VMEM] * (len(sizes) + 1),
            out_shape=[shape(size, width) for size in sizes] + [shape(hidden, count)],
            scratch_shapes=[pltpu.VMEM((count, width), BF16)],
            compiler_params=PARAMS,
            cost_estimate=cost
            or pl.CostEstimate(flops=4 * count * hidden * width, bytes_accessed=4000000, transcendentals=0),
        )(*rows, wt, cotangent)

    p2, m2 = shift(x0, 2), shift(x0, -2)
    far = shift(x0, 4)
    grad_held, grad_sent, onehot = pl.pallas_call(
        prepare_kernel,
        in_specs=[VMEM, VMEM],
        out_specs=[VMEM] * 3,
        out_shape=[
            shape(hidden, 128),
            shape(hidden, 128),
            jax.ShapeDtypeStruct((2, depth * n_nodes // 2, tok_grp), BF16),
        ],
        compiler_params=PARAMS,
    )(slots, grad)
    p2, grad_held, grad_sent, onehot = lax.optimization_barrier(
        (p2, grad_held, grad_sent, onehot)
    )
    to_p, to_m = pl.pallas_call(
        join_kernel,
        in_specs=[VMEM] * 3,
        out_specs=[VMEM] * 2,
        out_shape=[shape(64, width)] * 2,
        compiler_params=PARAMS,
        cost_estimate=WAIT,
    )(x0, p2, m2)
    p1, m1 = shift(to_p, 1), shift(to_m, -1)
    keep, to_far, dh_held = expert((x0, p2, m2, far), grad_held, (96, 32), WAIT)
    across = shift(to_far, 4)
    p1, keep, dh_held = lax.optimization_barrier((p1, keep, dh_held))
    to_m, to_p, dh_sent = expert((p1, m1), grad_sent, (64, 64))
    got_p, got_m = shift(to_p, 1), shift(to_m, -1)
    grad_wt = pl.pallas_call(
        weight_kernel,
        in_specs=[VMEM] * 8,
        out_specs=VMEM,
        out_shape=shape(hidden, width),
        scratch_shapes=[pltpu.VMEM((256, width), BF16), pltpu.VMEM((hidden, 256), BF16)],
        compiler_params=PARAMS,
        cost_estimate=pl.CostEstimate(flops=2 * 256 * hidden * width, bytes_accessed=5000000, transcendentals=0),
    )(dh_held, dh_sent, x0, p2, m2, p1, m1, far)
    near = pl.pallas_call(
        across_kernel,
        in_specs=[VMEM] * 2,
        out_specs=VMEM,
        out_shape=shape(32, width, F32),
        compiler_params=PARAMS,
        cost_estimate=WAIT,
    )(keep, across)
    got_p, got_m, near = lax.optimization_barrier((got_p, got_m, near))
    back_p, back_m = pl.pallas_call(
        middle_kernel,
        in_specs=[VMEM] * 3,
        out_specs=[VMEM] * 2,
        out_shape=[shape(32, width)] * 2,
        compiler_params=PARAMS,
        cost_estimate=WAIT,
    )(keep, got_p, got_m)
    from_p, from_m = shift(back_p, 2), shift(back_m, -2)
    from_p, from_m, grad_wt = lax.optimization_barrier((from_p, from_m, grad_wt))
    own_sum, other_sum = pl.pallas_call(
        last_kernel,
        in_specs=[VMEM] * 5,
        out_specs=[VMEM] * 2,
        out_shape=[shape(depth, width)] * 2,
        compiler_params=PARAMS,
    )(near, got_p, got_m, from_p, from_m)
    packed = pl.pallas_call(
        pack_kernel,
        in_specs=[VMEM] * 2,
        out_specs=VMEM,
        out_shape=jax.ShapeDtypeStruct((n_nodes, depth, 128), BF16),
        compiler_params=PARAMS,
    )(own_sum, swap(other_sum))
    arrived = lax.all_to_all(packed, "node", 0, 0, tiled=True)
    grad_xt = pl.pallas_call(
        spread_kernel,
        in_specs=[VMEM, VMEM],
        out_specs=VMEM,
        out_shape=shape(width // n_nodes, tok_grp, F32),
        compiler_params=PARAMS,
    )(onehot, arrived.reshape(n_nodes // 2, 2, depth, 128))
    return (grad_wt.T, grad_xt.T)


def solution(mesh):
    placed = (
        P(("dp", "chip"), None),
        P("dp", "chip", None, None),
        P(None, ("dp", "node", "chip")),
        P(None, ("dp", "node", "chip")),
    )
    return jax.shard_map(
        body,
        mesh=mesh,
        in_specs=placed,
        out_specs=(P(None, ("dp", "node", "chip")), P(("dp", "chip"), "node")),
        check_vma=False,
    )
```

time: 129 us -> 113 us (0.88); the launches traced: 126 us -> 112 us
  blocking collectives: 0 us -> 22.6 us
  waiting for transfers between devices: 35.6 us -> 13.9 us
  starting transfers between devices: 76.9 us -> 63.6 us
  local copies, waits for them, and re-layouts: 2.48 us -> 0.92 us
    all_to_all x0 -> x1, blocking collectives: none -> 22.6 us  [body(): arrived = lax.all_to_all(packed, 'node', 0, 0, tiled=True)]
    all_to_all x1 -> x0, starting transfers between devices: 14.3 us -> none  [body(): arrived = lax.all_to_all(packed, 'node', 0, 0, tiled=True)]
    all_to_all x1 -> x0, waiting for transfers between devices: 11.3 us -> none  [body(): arrived = lax.all_to_all(packed, 'node', 0, 0, tiled=True)]
    ppermute x12 -> x10, waiting for transfers between devices: 22.5 us -> 12.8 us  [shift(): lax.ppermute(value, 'chip', [(c, (c + by) % chips) for c in range(chips)])]
    ppermute x2, starting transfers between devices: 23.1 us -> 25.7 us  [swap(): return lax.ppermute(value, 'dp', [(0, 1), (1, 0)])]
    ppermute x12 -> x10, starting transfers between devices: 39.5 us -> 37.8 us  [shift(): lax.ppermute(value, 'chip', [(c, (c + by) % chips) for c in range(chips)])]
    unnamed x11 -> x7, local copies, waits for them, and re-layouts: 2.46 us -> 0.91 us
    pallas_call x3 -> x7, Pallas kernels: 7.35 us -> 8.02 us  [the longest x2 3.52 us: expert(): pl.pallas_call(functools.partial(expert_kernel, len(rows)), in_specs=[VME...]
  transfers between devices with their start and end apart: 15 -> 12, of which waited for: 8 -> 6; matrix products, arithmetic and copies ran while one was open for 0% -> 1% of each run, Pallas kernels for 1% -> 5%
where the time goes in v2:
time: 113 us; the launch traced here: 112 us
  starting transfers between devices  63.6 us (56%)
  blocking collectives  22.6 us (20%)
  waiting for transfers between devices  13.9 us (12%)
  Pallas kernels  10.2 us (9%)
    ppermute x10, starting transfers between devices, shift(): lax.ppermute(value, 'chip', [(c, (c + by) % chips) for c in range(chips)])  37.8 us
    ppermute x2, starting transfers between devices, swap(): return lax.ppermute(value, 'dp', [(0, 1), (1, 0)])  25.7 us
    all_to_all x1, blocking collectives, body(): arrived = lax.all_to_all(packed, 'node', 0, 0, tiled=True)  22.6 us
    ppermute x10, waiting for transfers between devices, shift(): lax.ppermute(value, 'chip', [(c, (c + by) % chips) for c in range(chips)])  12.8 us
    pallas_call x2, Pallas kernels, expert(): pl.pallas_call(functools.partial(expert_kernel, len(rows)), in_specs=[VME...  3.52 us
    pallas_call x1, Pallas kernels, body(): pl.pallas_call(pick_kernel, in_specs=[HBM] * 2, out_specs=[VMEM] * 2, out...  2.81 us
  transfers between devices with their start and end apart: 12, of which 6 were waited for; matrix products, arithmetic and copies ran while one was open for 1% of the time, Pallas kernels for 5%

profile of v2, /device:TPU:1, one launch (start us, length us, event | category | flops | bytes accessed | tf_op | source)
XLA Modules:
  0.0 112.0 jit_solution(1416268766709598378)
XLA Ops:
  0.6 2.8 %shard_map.59 = (bf16[16,2560]{1,0:T(8,128)(2,1)}, bf16[16,2560]{1,0:T(8,128)(2,1)}) custom-call(s32[16,64]{1,0:T(8,128)} %bitcast.12, bf16[512,2560]{1,0:T(8,128)(2,1)} %tokens_from.1), custom_call_target="tpu_custom_call" | custom-call | tf_op jit(solution)/shard_map/pallas_call | solution.py:193
  3.5 16.1 %collective-permute-start = (bf16[16,2560]{1,0:T(8,128)(2,1)}, bf16[16,2560]{1,0:T(8,128)(2,1)S(1)}, u32[]{:S(2)}, u32[]{:S(2)}) collective-permute-start(bf16[16,2560]{1,0:T(8,128)(2,1)} %get-tuple-element.33), channel_id=1, source_target_pairs={{0,512},{512,0},{1,513},{513,1},{2,514},{514,2},{3,515},{515,3},{4... | collective-permute-start | bytes 245768 | tf_op jit(solution)/shard_map/ppermute | solution.py:191
  19.5 0.9 constant_dynamic-update-slice_fusion.1
  20.4 0.2 collective-permute-done
  20.7 1.9 %collective-permute-start.1 = (bf16[32,2560]{1,0:T(8,128)(2,1)S(1)}, bf16[32,2560]{1,0:T(8,128)(2,1)S(1)}, u32[]{:S(2)}, u32[]{:S(2)}) collective-permute-start(bf16[32,2560]{1,0:T(8,128)(2,1)S(1)} %constant_dynamic-update-slice_fusion.x0.refs_0_), channel_id=1, source_target_pairs={{0,2},{1,3},{2,4},{3,5},{4,6},{5,7},{6,0},{7,1},{8,10},{9,11},{10,... | collective-permute-start | bytes 491528 | tf_op jit(solution)/shard_map/ppermute | solution.py:188
  22.6 5.5 %collective-permute-start.2 = (bf16[32,2560]{1,0:T(8,128)(2,1)S(1)}, bf16[32,2560]{1,0:T(8,128)(2,1)S(1)}, u32[]{:S(2)}, u32[]{:S(2)}) collective-permute-start(bf16[32,2560]{1,0:T(8,128)(2,1)S(1)} %constant_dynamic-update-slice_fusion.x0.refs_0_), channel_id=1, source_target_pairs={{0,6},{1,7},{2,0},{3,1},{4,2},{5,3},{6,4},{7,5},{8,14},{9,15},{10,... | collective-permute-start | bytes 491528 | tf_op jit(solution)/shard_map/ppermute | solution.py:188
  28.1 0.4 shard_map.60
  28.5 2.0 %collective-permute-start.4 = (bf16[32,2560]{1,0:T(8,128)(2,1)S(1)}, bf16[32,2560]{1,0:T(8,128)(2,1)S(1)}, u32[]{:S(2)}, u32[]{:S(2)}) collective-permute-start(bf16[32,2560]{1,0:T(8,128)(2,1)S(1)} %constant_dynamic-update-slice_fusion.x0.refs_0_), channel_id=1, source_target_pairs={{0,4},{1,5},{2,6},{3,7},{4,0},{5,1},{6,2},{7,3},{8,12},{9,13},{10,... | collective-permute-start | bytes 491528 | tf_op jit(solution)/shard_map/ppermute | solution.py:188
  30.5 0.0 collective-permute-done.1.p2.refs_1_
  30.5 0.0 copy-start
  30.5 2.6 %collective-permute-done.2.m2.refs_2_ = bf16[32,2560]{1,0:T(8,128)(2,1)S(1)} collective-permute-done((bf16[32,2560]{1,0:T(8,128)(2,1)S(1)}, bf16[32,2560]{1,0:T(8,128)(2,1)S(1)}, u32[]{:S(2)}, u32[]{:S(2)}) %collective-permute-start.2) | collective-permute-done | bytes 163872 | tf_op jit(solution)/shard_map/ppermute | solution.py:188
  33.2 4.0 %collective-permute-start.3 = (bf16[64,2560]{1,0:T(8,128)(2,1)S(1)}, bf16[64,2560]{1,0:T(8,128)(2,1)S(1)}, u32[]{:S(2)}, u32[]{:S(2)}) collective-permute-start(bf16[64,2560]{1,0:T(8,128)(2,1)S(1)} %get-tuple-element.38), channel_id=1, source_target_pairs={{0,1},{1,2},{2,3},{3,4},{4,5},{5,6},{6,7},{7,0},{8,9},{9,10},{10,1... | collective-permute-start | bytes 983048 | tf_op jit(solution)/shard_map/ppermute | solution.py:188
  37.2 7.1 %collective-permute-start.5 = (bf16[64,2560]{1,0:T(8,128)(2,1)S(1)}, bf16[64,2560]{1,0:T(8,128)(2,1)S(1)}, u32[]{:S(2)}, u32[]{:S(2)}) collective-permute-start(bf16[64,2560]{1,0:T(8,128)(2,1)S(1)} %get-tuple-element.44), channel_id=1, source_target_pairs={{0,7},{1,0},{2,1},{3,2},{4,3},{5,4},{6,5},{7,6},{8,15},{9,8},{10,9... | collective-permute-start | bytes 983048 | tf_op jit(solution)/shard_map/ppermute | solution.py:188
  44.3 1.8 %shard_map.62 = (bf16[96,2560]{1,0:T(8,128)(2,1)S(1)}, bf16[32,2560]{1,0:T(8,128)(2,1)S(1)}, bf16[320,128]{1,0:T(8,128)(2,1)S(1)}) custom-call(bf16[32,2560]{1,0:T(8,128)(2,1)S(1)} %constant_dynamic-update-slice_fusion.x0.refs_0_, bf16[32,2560]{1,0:T(8,128)(2,1)S(1)} %collective-permute-done.1.p2.refs_1_, ...), custom_call_target="tpu_custom_call" | custom-call | flops 20000000000 | tf_op jit(solution)/shard_map/pallas_call | solution.py:209
  46.1 2.9 %collective-permute-start.8 = (bf16[32,2560]{1,0:T(8,128)(2,1)S(1)}, bf16[32,2560]{1,0:T(8,128)(2,1)S(1)}, u32[]{:S(2)}, u32[]{:S(2)}) collective-permute-start(bf16[32,2560]{1,0:T(8,128)(2,1)S(1)} %get-tuple-element.48), channel_id=1, source_target_pairs={{0,4},{1,5},{2,6},{3,7},{4,0},{5,1},{6,2},{7,3},{8,12},{9,13},{10,... | collective-permute-start | bytes 491528 | tf_op jit(solution)/shard_map/ppermute | solution.py:188
  49.0 1.1 collective-permute-done.3.refs_0_.p1
  50.1 1.8 %shard_map.63 = (bf16[64,2560]{1,0:T(8,128)(2,1)S(1)}, bf16[64,2560]{1,0:T(8,128)(2,1)S(1)}, bf16[320,128]{1,0:T(8,128)(2,1)S(1)}) custom-call(bf16[64,2560]{1,0:T(8,128)(2,1)S(1)} %collective-permute-done.3.refs_0_.p1, bf16[64,2560]{1,0:T(8,128)(2,1)S(1)} %collective-permute-done.5.refs_1_.m1, bf16[320,2560]{1,0:T(8,128)(2,1)S(1)} %bitcast.9, ...), custom_call_target="tpu_custom_call" | custom-call | flops 419430400 | bytes 4000000 | tf_op jit(solution)/shard_map/pallas_call | solution.py:209
  51.9 3.9 %collective-permute-start.6 = (bf16[64,2560]{1,0:T(8,128)(2,1)S(1)}, bf16[64,2560]{1,0:T(8,128)(2,1)S(1)}, u32[]{:S(2)}, u32[]{:S(2)}) collective-permute-start(bf16[64,2560]{1,0:T(8,128)(2,1)S(1)} %get-tuple-element.46), channel_id=1, source_target_pairs={{0,1},{1,2},{2,3},{3,4},{4,5},{5,6},{6,7},{7,0},{8,9},{9,10},{10,1... | collective-permute-start | bytes 983048 | tf_op jit(solution)/shard_map/ppermute | solution.py:188
  55.8 3.1 %collective-permute-start.7 = (bf16[64,2560]{1,0:T(8,128)(2,1)S(1)}, bf16[64,2560]{1,0:T(8,128)(2,1)S(1)}, u32[]{:S(2)}, u32[]{:S(2)}) collective-permute-start(bf16[64,2560]{1,0:T(8,128)(2,1)S(1)} %get-tuple-element.47), channel_id=1, source_target_pairs={{0,7},{1,0},{2,1},{3,2},{4,3},{5,4},{6,5},{7,6},{8,15},{9,8},{10,9... | collective-permute-start | bytes 983048 | tf_op jit(solution)/shard_map/ppermute | solution.py:188
  58.9 0.0 collective-permute-done.8.across
  59.0 7.2 %collective-permute-done.6.got_p = bf16[64,2560]{1,0:T(8,128)(2,1)S(1)} collective-permute-done((bf16[64,2560]{1,0:T(8,128)(2,1)S(1)}, bf16[64,2560]{1,0:T(8,128)(2,1)S(1)}, u32[]{:S(2)}, u32[]{:S(2)}) %collective-permute-start.6) | collective-permute-done | bytes 327712 | tf_op jit(solution)/shard_map/ppermute | solution.py:188
  66.2 0.1 shard_map.65
  66.3 2.8 %collective-permute-start.9 = (bf16[32,2560]{1,0:T(8,128)(2,1)S(1)}, bf16[32,2560]{1,0:T(8,128)(2,1)S(1)}, u32[]{:S(2)}, u32[]{:S(2)}) collective-permute-start(bf16[32,2560]{1,0:T(8,128)(2,1)S(1)} %get-tuple-element.51), channel_id=1, source_target_pairs={{0,2},{1,3},{2,4},{3,5},{4,6},{5,7},{6,0},{7,1},{8,10},{9,11},{10,... | collective-permute-start | bytes 491528 | tf_op jit(solution)/shard_map/ppermute | solution.py:188
  69.1 4.6 %collective-permute-start.10 = (bf16[32,2560]{1,0:T(8,128)(2,1)S(1)}, bf16[32,2560]{1,0:T(8,128)(2,1)S(1)}, u32[]{:S(2)}, u32[]{:S(2)}) collective-permute-start(bf16[32,2560]{1,0:T(8,128)(2,1)S(1)} %get-tuple-element.52), channel_id=1, source_target_pairs={{0,6},{1,7},{2,0},{3,1},{4,2},{5,3},{6,4},{7,5},{8,14},{9,15},{10,... | collective-permute-start | bytes 491528 | tf_op jit(solution)/shard_map/ppermute | solution.py:188
  73.7 1.8 %shard_map.66 = bf16[320,2560]{1,0:T(8,128)(2,1)} custom-call(bf16[320,128]{1,0:T(8,128)(2,1)S(1)} %get-tuple-element.53.dh_held, bf16[320,128]{1,0:T(8,128)(2,1)S(1)} %get-tuple-element.54.dh_sent, bf16[32,2560]{1,0:T(8,128)(2,1)S(1)} %constant_dynamic-update-slice_fusion.x0.refs_0_, bf16[32,2560]{1,0:T(8,128)(2,1)S(1)} %collective-permute-done.1.p2.refs_1_, ...), custom_call_target="tpu_custom_call" | custom-call | flops 419430400 | bytes 5000000 | tf_op jit(solution)/shard_map/pallas_call | solution.py:250
  75.4 1.9 %collective-permute-done.10.from_m = bf16[32,2560]{1,0:T(8,128)(2,1)S(1)} collective-permute-done((bf16[32,2560]{1,0:T(8,128)(2,1)S(1)}, bf16[32,2560]{1,0:T(8,128)(2,1)S(1)}, u32[]{:S(2)}, u32[]{:S(2)}) %collective-permute-start.10) | collective-permute-done | bytes 163872 | tf_op jit(solution)/shard_map/ppermute | solution.py:188
  77.3 0.1 shard_map.67
  77.4 9.7 %collective-permute-start.11 = (bf16[16,2560]{1,0:T(8,128)(2,1)S(1)}, bf16[16,2560]{1,0:T(8,128)(2,1)S(1)}, u32[]{:S(2)}, u32[]{:S(2)}) collective-permute-start(bf16[16,2560]{1,0:T(8,128)(2,1)S(1)} %get-tuple-element.61), channel_id=1, source_target_pairs={{0,512},{512,0},{1,513},{513,1},{2,514},{514,2},{3,515},{515,3},{4... | collective-permute-start | bytes 245768 | tf_op jit(solution)/shard_map/ppermute | solution.py:191
  87.1 0.9 collective-permute-done.11.other
  88.0 0.2 shard_map.68
  88.2 22.6 %all_to_all.5 = bf16[64,16,128]{2,1,0:T(8,128)(2,1)S(1)} all-to-all(bf16[64,16,128]{2,1,0:T(8,128)(2,1)S(1)} %shard_map.68), channel_id=1, replica_groups=mesh['dp'=2,'node'=64,'chip'=8] {'node'}, dimensions={0} | all-to-all | bytes 524288 | tf_op jit(solution)/shard_map/all_to_all | solution.py:292
  110.8 1.2 %shard_map.69 = f32[40,512]{1,0:T(8,128)} custom-call(bf16[2,512,512]{2,1,0:T(8,128)(2,1)S(1)} %get-tuple-element.56.onehot, bf16[32,2,16,128]{3,2,1,0:T(8,128)(2,1)S(1)} %bitcast.10), custom_call_target="tpu_custom_call" | custom-call | tf_op jit(solution)/shard_map/pallas_call | solution.py:293
  (12 shorter events, 0.1 us)
Async XLA Ops:
  0.6 27.4 %copy-start.2 = (s32[1,1,64,16]{2,3,1,0:T(8,128)S(1)}, s32[1,1,64,16]{2,3,1,0:T(8,128)}, u32[]{:S(2)}) copy-start(s32[1,1,64,16]{2,3,1,0:T(8,128)} %param.5) | copy-start | bytes 12292
  0.6 27.4 %copy-start.1 = (bf16[256,320]{0,1:T(8,128)(2,1)S(1)}, bf16[256,320]{0,1:T(8,128)(2,1)}, u32[]{:S(2)}) copy-start(bf16[256,320]{0,1:T(8,128)(2,1)} %param.6) | copy-start | bytes 491524
  3.5 17.2 %collective-permute-start = (bf16[16,2560]{1,0:T(8,128)(2,1)}, bf16[16,2560]{1,0:T(8,128)(2,1)S(1)}, u32[]{:S(2)}, u32[]{:S(2)}) collective-permute-start(bf16[16,2560]{1,0:T(8,128)(2,1)} %get-tuple-element.33), channel_id=1, source_target_pairs={{0,512},{512,0},{1,513},{513,1},{2,514},{514,2},{3,515},{515,3},{4... | collective-permute-start | bytes 245768 | tf_op jit(solution)/shard_map/ppermute | solution.py:191
  20.7 9.9 %collective-permute-start.1 = (bf16[32,2560]{1,0:T(8,128)(2,1)S(1)}, bf16[32,2560]{1,0:T(8,128)(2,1)S(1)}, u32[]{:S(2)}, u32[]{:S(2)}) collective-permute-start(bf16[32,2560]{1,0:T(8,128)(2,1)S(1)} %constant_dynamic-update-slice_fusion.x0.refs_0_), channel_id=1, source_target_pairs={{0,2},{1,3},{2,4},{3,5},{4,6},{5,7},{6,0},{7,1},{8,10},{9,11},{10,... | collective-permute-start | bytes 491528 | tf_op jit(solution)/shard_map/ppermute | solution.py:188
  22.6 10.6 %collective-permute-start.2 = (bf16[32,2560]{1,0:T(8,128)(2,1)S(1)}, bf16[32,2560]{1,0:T(8,128)(2,1)S(1)}, u32[]{:S(2)}, u32[]{:S(2)}) collective-permute-start(bf16[32,2560]{1,0:T(8,128)(2,1)S(1)} %constant_dynamic-update-slice_fusion.x0.refs_0_), channel_id=1, source_target_pairs={{0,6},{1,7},{2,0},{3,1},{4,2},{5,3},{6,4},{7,5},{8,14},{9,15},{10,... | collective-permute-start | bytes 491528 | tf_op jit(solution)/shard_map/ppermute | solution.py:188
  28.5 15.8 %collective-permute-start.4 = (bf16[32,2560]{1,0:T(8,128)(2,1)S(1)}, bf16[32,2560]{1,0:T(8,128)(2,1)S(1)}, u32[]{:S(2)}, u32[]{:S(2)}) collective-permute-start(bf16[32,2560]{1,0:T(8,128)(2,1)S(1)} %constant_dynamic-update-slice_fusion.x0.refs_0_), channel_id=1, source_target_pairs={{0,4},{1,5},{2,6},{3,7},{4,0},{5,1},{6,2},{7,3},{8,12},{9,13},{10,... | collective-permute-start | bytes 491528 | tf_op jit(solution)/shard_map/ppermute | solution.py:188
  30.5 13.8 %copy-start = (bf16[2560,320]{0,1:T(8,128)(2,1)S(1)}, bf16[2560,320]{0,1:T(8,128)(2,1)}, u32[]{:S(2)}) copy-start(bf16[2560,320]{0,1:T(8,128)(2,1)} %param.7) | copy-start | bytes 4915204
  33.2 16.9 %collective-permute-start.3 = (bf16[64,2560]{1,0:T(8,128)(2,1)S(1)}, bf16[64,2560]{1,0:T(8,128)(2,1)S(1)}, u32[]{:S(2)}, u32[]{:S(2)}) collective-permute-start(bf16[64,2560]{1,0:T(8,128)(2,1)S(1)} %get-tuple-element.38), channel_id=1, source_target_pairs={{0,1},{1,2},{2,3},{3,4},{4,5},{5,6},{6,7},{7,0},{8,9},{9,10},{10,1... | collective-permute-start | bytes 983048 | tf_op jit(solution)/shard_map/ppermute | solution.py:188
  37.2 12.9 %collective-permute-start.5 = (bf16[64,2560]{1,0:T(8,128)(2,1)S(1)}, bf16[64,2560]{1,0:T(8,128)(2,1)S(1)}, u32[]{:S(2)}, u32[]{:S(2)}) collective-permute-start(bf16[64,2560]{1,0:T(8,128)(2,1)S(1)} %get-tuple-element.44), channel_id=1, source_target_pairs={{0,7},{1,0},{2,1},{3,2},{4,3},{5,4},{6,5},{7,6},{8,15},{9,8},{10,9... | collective-permute-start | bytes 983048 | tf_op jit(solution)/shard_map/ppermute | solution.py:188
  46.1 12.8 %collective-permute-start.8 = (bf16[32,2560]{1,0:T(8,128)(2,1)S(1)}, bf16[32,2560]{1,0:T(8,128)(2,1)S(1)}, u32[]{:S(2)}, u32[]{:S(2)}) collective-permute-start(bf16[32,2560]{1,0:T(8,128)(2,1)S(1)} %get-tuple-element.48), channel_id=1, source_target_pairs={{0,4},{1,5},{2,6},{3,7},{4,0},{5,1},{6,2},{7,3},{8,12},{9,13},{10,... | collective-permute-start | bytes 491528 | tf_op jit(solution)/shard_map/ppermute | solution.py:188
  51.9 14.3 %collective-permute-start.6 = (bf16[64,2560]{1,0:T(8,128)(2,1)S(1)}, bf16[64,2560]{1,0:T(8,128)(2,1)S(1)}, u32[]{:S(2)}, u32[]{:S(2)}) collective-permute-start(bf16[64,2560]{1,0:T(8,128)(2,1)S(1)} %get-tuple-element.46), channel_id=1, source_target_pairs={{0,1},{1,2},{2,3},{3,4},{4,5},{5,6},{6,7},{7,0},{8,9},{9,10},{10,1... | collective-permute-start | bytes 983048 | tf_op jit(solution)/shard_map/ppermute | solution.py:188
  55.8 10.4 %collective-permute-start.7 = (bf16[64,2560]{1,0:T(8,128)(2,1)S(1)}, bf16[64,2560]{1,0:T(8,128)(2,1)S(1)}, u32[]{:S(2)}, u32[]{:S(2)}) collective-permute-start(bf16[64,2560]{1,0:T(8,128)(2,1)S(1)} %get-tuple-element.47), channel_id=1, source_target_pairs={{0,7},{1,0},{2,1},{3,2},{4,3},{5,4},{6,5},{7,6},{8,15},{9,8},{10,9... | collective-permute-start | bytes 983048 | tf_op jit(solution)/shard_map/ppermute | solution.py:188
  66.3 9.2 %collective-permute-start.9 = (bf16[32,2560]{1,0:T(8,128)(2,1)S(1)}, bf16[32,2560]{1,0:T(8,128)(2,1)S(1)}, u32[]{:S(2)}, u32[]{:S(2)}) collective-permute-start(bf16[32,2560]{1,0:T(8,128)(2,1)S(1)} %get-tuple-element.51), channel_id=1, source_target_pairs={{0,2},{1,3},{2,4},{3,5},{4,6},{5,7},{6,0},{7,1},{8,10},{9,11},{10,... | collective-permute-start | bytes 491528 | tf_op jit(solution)/shard_map/ppermute | solution.py:188
  69.1 8.3 %collective-permute-start.10 = (bf16[32,2560]{1,0:T(8,128)(2,1)S(1)}, bf16[32,2560]{1,0:T(8,128)(2,1)S(1)}, u32[]{:S(2)}, u32[]{:S(2)}) collective-permute-start(bf16[32,2560]{1,0:T(8,128)(2,1)S(1)} %get-tuple-element.52), channel_id=1, source_target_pairs={{0,6},{1,7},{2,0},{3,1},{4,2},{5,3},{6,4},{7,5},{8,14},{9,15},{10,... | collective-permute-start | bytes 491528 | tf_op jit(solution)/shard_map/ppermute | solution.py:188
  77.4 10.6 %collective-permute-start.11 = (bf16[16,2560]{1,0:T(8,128)(2,1)S(1)}, bf16[16,2560]{1,0:T(8,128)(2,1)S(1)}, u32[]{:S(2)}, u32[]{:S(2)}) collective-permute-start(bf16[16,2560]{1,0:T(8,128)(2,1)S(1)} %get-tuple-element.61), channel_id=1, source_target_pairs={{0,512},{512,0},{1,513},{513,1},{2,514},{514,2},{3,515},{515,3},{4... | collective-permute-start | bytes 245768 | tf_op jit(solution)/shard_map/ppermute | solution.py:191

commit v3 on v2

--- a/solution.py
+++ b/solution.py
@@ -78,8 +78,7 @@
     tokens = onehot.shape[2]
     token = lax.broadcasted_iota(jnp.int32, (depth, tokens), 1)
     for half in range(2):
-        swap = lax.rem(dp + half, 2)
-        listed = jnp.where(swap == 0, slots[:, :experts], slots[:, experts:])
+        listed = slots[:, half * experts : (half + 1) * experts]
         for expert in range(experts):
             column = listed[:, expert : expert + 1]
             onehot[half, expert * depth : (expert + 1) * depth, :] = jnp.where(
@@ -150,20 +149,24 @@
 
 
 def pack_kernel(own, other, out):
-    nodes = out.shape[0]
+    dp = lax.axis_index("dp")
+    nodes = out.shape[1]
     wide = own.shape[1] // nodes
-    gap = jnp.zeros((own.shape[0], 64 - wide), BF16)
+    gap = jnp.zeros((own.shape[0], 128 - wide), BF16)
+    low = jnp.where(dp == 0, own[...], other[...])
+    high = jnp.where(dp == 0, other[...], own[...])
     for node in range(nodes):
         cols = slice(node * wide, (node + 1) * wide)
-        out[node] = jnp.concatenate([own[:, cols], gap, other[:, cols], gap], axis=1)
+        out[0, node] = jnp.concatenate([low[:, cols], gap], axis=1)
+        out[1, node] = jnp.concatenate([high[:, cols], gap], axis=1)
 
 
 def spread_kernel(onehot, arrived, out):
     wide, tokens = out.shape
-    total = jnp.zeros((64, tokens), F32)
+    total = jnp.zeros((128, tokens), F32)
     for half in range(2):
         for pair in range(2):
-            got = arrived[:, pair, :, half * 64 : half * 64 + 64].reshape(onehot.shape[1], 64)
+            got = arrived[half, :, pair].reshape(onehot.shape[1], 128)
             total += lax.dot_general(
                 got, onehot[half], (((0,), (0,)), ((), ())), preferred_element_type=F32
             )
@@ -286,17 +289,19 @@
         pack_kernel,
         in_specs=[VMEM] * 2,
         out_specs=VMEM,
-        out_shape=jax.ShapeDtypeStruct((n_nodes, depth, 128), BF16),
-        compiler_params=PARAMS,
-    )(own_sum, swap(other_sum))
-    arrived = lax.all_to_all(packed, "node", 0, 0, tiled=True)
+        out_shape=jax.ShapeDtypeStruct((2, n_nodes, depth, 128), BF16),
+        compiler_params=PARAMS,
+    )(own_sum, other_sum)
+    arrived = lax.all_to_all(
+        packed.reshape(2 * n_nodes, depth, 128), ("dp", "node"), 0, 0, tiled=True
+    )
     grad_xt = pl.pallas_call(
         spread_kernel,
         in_specs=[VMEM, VMEM],
         out_specs=VMEM,
         out_shape=shape(width // n_nodes, tok_grp, F32),
         compiler_params=PARAMS,
-    )(onehot, arrived.reshape(n_nodes // 2, 2, depth, 128))
+    )(onehot, arrived.reshape(2, n_nodes // 2, 2, depth, 128))
     return (grad_wt.T, grad_xt.T)
 
 

time: 113 us -> 118 us (1.044)
  blocking collectives: 22.6 us -> 38.1 us
  starting transfers between devices: 63.6 us -> 54.1 us
    all_to_all x1, blocking collectives: 22.6 us -> 38.1 us  [body(): lax.all_to_all(packed.reshape(2 * n_nodes, depth, 128), ('dp', 'node'), 0...]
    ppermute x2 -> x1, starting transfers between devices: 25.7 us -> 16.1 us  [swap(): return lax.ppermute(value, 'dp', [(0, 1), (1, 0)])]
  transfers between devices with their start and end apart: 12 -> 11, of which waited for: 6 -> 7; matrix products, arithmetic and copies ran while one was open for 1% -> 1% of each run, Pallas kernels for 5% -> 5%
where the time goes in v3:
time: 118 us
  starting transfers between devices  54.1 us (46%)
  blocking collectives  38.1 us (32%)
  waiting for transfers between devices  13.9 us (12%)
  Pallas kernels  9.96 us (8%)
    all_to_all x1, blocking collectives, body(): lax.all_to_all(packed.reshape(2 * n_nodes, depth, 128), ('dp', 'node'), 0...  38.1 us
    ppermute x10, starting transfers between devices, shift(): lax.ppermute(value, 'chip', [(c, (c + by) % chips) for c in range(chips)])  38 us
    ppermute x1, starting transfers between devices, swap(): return lax.ppermute(value, 'dp', [(0, 1), (1, 0)])  16.1 us
    ppermute x10, waiting for transfers between devices, shift(): lax.ppermute(value, 'chip', [(c, (c + by) % chips) for c in range(chips)])  13.7 us
    pallas_call x2, Pallas kernels, expert(): pl.pallas_call(functools.partial(expert_kernel, len(rows)), in_specs=[VME...  3.52 us
    pallas_call x1, Pallas kernels, body(): pl.pallas_call(pick_kernel, in_specs=[HBM] * 2, out_specs=[VMEM] * 2, out...  2.81 us
  transfers between devices with their start and end apart: 11, of which 7 were waited for; matrix products, arithmetic and copies ran while one was open for 1% of the time, Pallas kernels for 5%

profile of v3, /device:TPU:1, one launch (start us, length us, event | category | flops | bytes accessed | tf_op | source)
XLA Modules:
  0.0 117.7 jit_solution(4990328936499353737)
XLA Ops:
  0.6 2.8 %shard_map.59 = (bf16[16,2560]{1,0:T(8,128)(2,1)}, bf16[16,2560]{1,0:T(8,128)(2,1)}) custom-call(s32[16,64]{1,0:T(8,128)} %bitcast.14, bf16[512,2560]{1,0:T(8,128)(2,1)} %tokens_from.1), custom_call_target="tpu_custom_call" | custom-call | tf_op jit(solution)/shard_map/pallas_call | solution.py:196
  3.5 16.1 %collective-permute-start = (bf16[16,2560]{1,0:T(8,128)(2,1)}, bf16[16,2560]{1,0:T(8,128)(2,1)S(1)}, u32[]{:S(2)}, u32[]{:S(2)}) collective-permute-start(bf16[16,2560]{1,0:T(8,128)(2,1)} %get-tuple-element.33), channel_id=1, source_target_pairs={{0,512},{512,0},{1,513},{513,1},{2,514},{514,2},{3,515},{515,3},{4... | collective-permute-start | bytes 245768 | tf_op jit(solution)/shard_map/ppermute | solution.py:194
  19.5 0.9 constant_dynamic-update-slice_fusion.1
  20.4 0.2 collective-permute-done
  20.7 1.9 %collective-permute-start.1 = (bf16[32,2560]{1,0:T(8,128)(2,1)S(1)}, bf16[32,2560]{1,0:T(8,128)(2,1)S(1)}, u32[]{:S(2)}, u32[]{:S(2)}) collective-permute-start(bf16[32,2560]{1,0:T(8,128)(2,1)S(1)} %constant_dynamic-update-slice_fusion.x0.refs_0_), channel_id=1, source_target_pairs={{0,2},{1,3},{2,4},{3,5},{4,6},{5,7},{6,0},{7,1},{8,10},{9,11},{10,... | collective-permute-start | bytes 491528 | tf_op jit(solution)/shard_map/ppermute | solution.py:191
  22.6 5.5 %collective-permute-start.2 = (bf16[32,2560]{1,0:T(8,128)(2,1)S(1)}, bf16[32,2560]{1,0:T(8,128)(2,1)S(1)}, u32[]{:S(2)}, u32[]{:S(2)}) collective-permute-start(bf16[32,2560]{1,0:T(8,128)(2,1)S(1)} %constant_dynamic-update-slice_fusion.x0.refs_0_), channel_id=1, source_target_pairs={{0,6},{1,7},{2,0},{3,1},{4,2},{5,3},{6,4},{7,5},{8,14},{9,15},{10,... | collective-permute-start | bytes 491528 | tf_op jit(solution)/shard_map/ppermute | solution.py:191
  28.1 0.3 shard_map.60
  28.4 2.0 %collective-permute-start.4 = (bf16[32,2560]{1,0:T(8,128)(2,1)S(1)}, bf16[32,2560]{1,0:T(8,128)(2,1)S(1)}, u32[]{:S(2)}, u32[]{:S(2)}) collective-permute-start(bf16[32,2560]{1,0:T(8,128)(2,1)S(1)} %constant_dynamic-update-slice_fusion.x0.refs_0_), channel_id=1, source_target_pairs={{0,4},{1,5},{2,6},{3,7},{4,0},{5,1},{6,2},{7,3},{8,12},{9,13},{10,... | collective-permute-start | bytes 491528 | tf_op jit(solution)/shard_map/ppermute | solution.py:191
  30.4 0.0 collective-permute-done.1.p2.refs_1_
  30.4 0.0 copy-start
  30.4 2.8 %collective-permute-done.2.m2.refs_2_ = bf16[32,2560]{1,0:T(8,128)(2,1)S(1)} collective-permute-done((bf16[32,2560]{1,0:T(8,128)(2,1)S(1)}, bf16[32,2560]{1,0:T(8,128)(2,1)S(1)}, u32[]{:S(2)}, u32[]{:S(2)}) %collective-permute-start.2) | collective-permute-done | bytes 163872 | tf_op jit(solution)/shard_map/ppermute | solution.py:191
  33.2 4.0 %collective-permute-start.3 = (bf16[64,2560]{1,0:T(8,128)(2,1)S(1)}, bf16[64,2560]{1,0:T(8,128)(2,1)S(1)}, u32[]{:S(2)}, u32[]{:S(2)}) collective-permute-start(bf16[64,2560]{1,0:T(8,128)(2,1)S(1)} %get-tuple-element.38), channel_id=1, source_target_pairs={{0,1},{1,2},{2,3},{3,4},{4,5},{5,6},{6,7},{7,0},{8,9},{9,10},{10,1... | collective-permute-start | bytes 983048 | tf_op jit(solution)/shard_map/ppermute | solution.py:191
  37.2 7.4 %collective-permute-start.5 = (bf16[64,2560]{1,0:T(8,128)(2,1)S(1)}, bf16[64,2560]{1,0:T(8,128)(2,1)S(1)}, u32[]{:S(2)}, u32[]{:S(2)}) collective-permute-start(bf16[64,2560]{1,0:T(8,128)(2,1)S(1)} %get-tuple-element.44), channel_id=1, source_target_pairs={{0,7},{1,0},{2,1},{3,2},{4,3},{5,4},{6,5},{7,6},{8,15},{9,8},{10,9... | collective-permute-start | bytes 983048 | tf_op jit(solution)/shard_map/ppermute | solution.py:191
  44.6 0.0 collective-permute-done.4.refs_3_.far
  44.6 1.8 %shard_map.62 = (bf16[96,2560]{1,0:T(8,128)(2,1)S(1)}, bf16[32,2560]{1,0:T(8,128)(2,1)S(1)}, bf16[320,128]{1,0:T(8,128)(2,1)S(1)}) custom-call(bf16[32,2560]{1,0:T(8,128)(2,1)S(1)} %constant_dynamic-update-slice_fusion.x0.refs_0_, bf16[32,2560]{1,0:T(8,128)(2,1)S(1)} %collective-permute-done.1.p2.refs_1_, ...), custom_call_target="tpu_custom_call" | custom-call | flops 20000000000 | tf_op jit(solution)/shard_map/pallas_call | solution.py:212
  46.4 2.6 %collective-permute-start.8 = (bf16[32,2560]{1,0:T(8,128)(2,1)S(1)}, bf16[32,2560]{1,0:T(8,128)(2,1)S(1)}, u32[]{:S(2)}, u32[]{:S(2)}) collective-permute-start(bf16[32,2560]{1,0:T(8,128)(2,1)S(1)} %get-tuple-element.48), channel_id=1, source_target_pairs={{0,4},{1,5},{2,6},{3,7},{4,0},{5,1},{6,2},{7,3},{8,12},{9,13},{10,... | collective-permute-start | bytes 491528 | tf_op jit(solution)/shard_map/ppermute | solution.py:191
  49.0 0.7 collective-permute-done.3.refs_0_.p1
  49.7 0.7 collective-permute-done.5.refs_1_.m1
  50.3 1.8 %shard_map.63 = (bf16[64,2560]{1,0:T(8,128)(2,1)S(1)}, bf16[64,2560]{1,0:T(8,128)(2,1)S(1)}, bf16[320,128]{1,0:T(8,128)(2,1)S(1)}) custom-call(bf16[64,2560]{1,0:T(8,128)(2,1)S(1)} %collective-permute-done.3.refs_0_.p1, bf16[64,2560]{1,0:T(8,128)(2,1)S(1)} %collective-permute-done.5.refs_1_.m1, bf16[320,2560]{1,0:T(8,128)(2,1)S(1)} %bitcast.12, ...), custom_call_target="tpu_custom_call" | custom-call | flops 419430400 | bytes 4000000 | tf_op jit(solution)/shard_map/pallas_call | solution.py:212
  52.1 3.7 %collective-permute-start.6 = (bf16[64,2560]{1,0:T(8,128)(2,1)S(1)}, bf16[64,2560]{1,0:T(8,128)(2,1)S(1)}, u32[]{:S(2)}, u32[]{:S(2)}) collective-permute-start(bf16[64,2560]{1,0:T(8,128)(2,1)S(1)} %get-tuple-element.46), channel_id=1, source_target_pairs={{0,1},{1,2},{2,3},{3,4},{4,5},{5,6},{6,7},{7,0},{8,9},{9,10},{10,1... | collective-permute-start | bytes 983048 | tf_op jit(solution)/shard_map/ppermute | solution.py:191
  55.8 3.6 %collective-permute-start.7 = (bf16[64,2560]{1,0:T(8,128)(2,1)S(1)}, bf16[64,2560]{1,0:T(8,128)(2,1)S(1)}, u32[]{:S(2)}, u32[]{:S(2)}) collective-permute-start(bf16[64,2560]{1,0:T(8,128)(2,1)S(1)} %get-tuple-element.47), channel_id=1, source_target_pairs={{0,7},{1,0},{2,1},{3,2},{4,3},{5,4},{6,5},{7,6},{8,15},{9,8},{10,9... | collective-permute-start | bytes 983048 | tf_op jit(solution)/shard_map/ppermute | solution.py:191
  59.4 7.4 %collective-permute-done.6.got_p = bf16[64,2560]{1,0:T(8,128)(2,1)S(1)} collective-permute-done((bf16[64,2560]{1,0:T(8,128)(2,1)S(1)}, bf16[64,2560]{1,0:T(8,128)(2,1)S(1)}, u32[]{:S(2)}, u32[]{:S(2)}) %collective-permute-start.6) | collective-permute-done | bytes 327712 | tf_op jit(solution)/shard_map/ppermute | solution.py:191
  66.8 0.1 shard_map.65
  66.9 2.2 %collective-permute-start.9 = (bf16[32,2560]{1,0:T(8,128)(2,1)S(1)}, bf16[32,2560]{1,0:T(8,128)(2,1)S(1)}, u32[]{:S(2)}, u32[]{:S(2)}) collective-permute-start(bf16[32,2560]{1,0:T(8,128)(2,1)S(1)} %get-tuple-element.51), channel_id=1, source_target_pairs={{0,2},{1,3},{2,4},{3,5},{4,6},{5,7},{6,0},{7,1},{8,10},{9,11},{10,... | collective-permute-start | bytes 491528 | tf_op jit(solution)/shard_map/ppermute | solution.py:191
  69.1 5.2 %collective-permute-start.10 = (bf16[32,2560]{1,0:T(8,128)(2,1)S(1)}, bf16[32,2560]{1,0:T(8,128)(2,1)S(1)}, u32[]{:S(2)}, u32[]{:S(2)}) collective-permute-start(bf16[32,2560]{1,0:T(8,128)(2,1)S(1)} %get-tuple-element.52), channel_id=1, source_target_pairs={{0,6},{1,7},{2,0},{3,1},{4,2},{5,3},{6,4},{7,5},{8,14},{9,15},{10,... | collective-permute-start | bytes 491528 | tf_op jit(solution)/shard_map/ppermute | solution.py:191
  74.3 1.8 %shard_map.66 = bf16[320,2560]{1,0:T(8,128)(2,1)} custom-call(bf16[320,128]{1,0:T(8,128)(2,1)S(1)} %get-tuple-element.53.dh_held, bf16[320,128]{1,0:T(8,128)(2,1)S(1)} %get-tuple-element.54.dh_sent, bf16[32,2560]{1,0:T(8,128)(2,1)S(1)} %constant_dynamic-update-slice_fusion.x0.refs_0_, bf16[32,2560]{1,0:T(8,128)(2,1)S(1)} %collective-permute-done.1.p2.refs_1_, ...), custom_call_target="tpu_custom_call" | custom-call | flops 419430400 | bytes 5000000 | tf_op jit(solution)/shard_map/pallas_call | solution.py:253
  76.0 0.8 collective-permute-done.9.from_p
  76.8 1.5 %collective-permute-done.10.from_m = bf16[32,2560]{1,0:T(8,128)(2,1)S(1)} collective-permute-done((bf16[32,2560]{1,0:T(8,128)(2,1)S(1)}, bf16[32,2560]{1,0:T(8,128)(2,1)S(1)}, u32[]{:S(2)}, u32[]{:S(2)}) %collective-permute-start.10) | collective-permute-done | bytes 163872 | tf_op jit(solution)/shard_map/ppermute | solution.py:191
  78.3 0.1 shard_map.67
  78.4 0.2 shard_map.68
  78.6 38.1 %all_to_all.5 = bf16[128,16,128]{2,1,0:T(8,128)(2,1)S(1)} all-to-all(bf16[128,16,128]{2,1,0:T(8,128)(2,1)S(1)} %bitcast.10), channel_id=1, replica_groups=mesh['dp'=2,'node'=64,'chip'=8] {'dp','node'}, dimensions={0} | all-to-all | bytes 1048576 | tf_op jit(solution)/shard_map/all_to_all | solution.py:295
  116.7 1.1 shard_map.69
  (10 shorter events, 0.1 us)
Async XLA Ops:
  0.6 27.4 %copy-start.2 = (s32[1,1,64,16]{2,3,1,0:T(8,128)S(1)}, s32[1,1,64,16]{2,3,1,0:T(8,128)}, u32[]{:S(2)}) copy-start(s32[1,1,64,16]{2,3,1,0:T(8,128)} %param.5) | copy-start | bytes 12292
  0.6 27.4 %copy-start.1 = (bf16[256,320]{0,1:T(8,128)(2,1)S(1)}, bf16[256,320]{0,1:T(8,128)(2,1)}, u32[]{:S(2)}) copy-start(bf16[256,320]{0,1:T(8,128)(2,1)} %param.6) | copy-start | bytes 491524
  3.5 17.2 %collective-permute-start = (bf16[16,2560]{1,0:T(8,128)(2,1)}, bf16[16,2560]{1,0:T(8,128)(2,1)S(1)}, u32[]{:S(2)}, u32[]{:S(2)}) collective-permute-start(bf16[16,2560]{1,0:T(8,128)(2,1)} %get-tuple-element.33), channel_id=1, source_target_pairs={{0,512},{512,0},{1,513},{513,1},{2,514},{514,2},{3,515},{515,3},{4... | collective-permute-start | bytes 245768 | tf_op jit(solution)/shard_map/ppermute | solution.py:194
  20.7 9.7 %collective-permute-start.1 = (bf16[32,2560]{1,0:T(8,128)(2,1)S(1)}, bf16[32,2560]{1,0:T(8,128)(2,1)S(1)}, u32[]{:S(2)}, u32[]{:S(2)}) collective-permute-start(bf16[32,2560]{1,0:T(8,128)(2,1)S(1)} %constant_dynamic-update-slice_fusion.x0.refs_0_), channel_id=1, source_target_pairs={{0,2},{1,3},{2,4},{3,5},{4,6},{5,7},{6,0},{7,1},{8,10},{9,11},{10,... | collective-permute-start | bytes 491528 | tf_op jit(solution)/shard_map/ppermute | solution.py:191
  22.6 10.6 %collective-permute-start.2 = (bf16[32,2560]{1,0:T(8,128)(2,1)S(1)}, bf16[32,2560]{1,0:T(8,128)(2,1)S(1)}, u32[]{:S(2)}, u32[]{:S(2)}) collective-permute-start(bf16[32,2560]{1,0:T(8,128)(2,1)S(1)} %constant_dynamic-update-slice_fusion.x0.refs_0_), channel_id=1, source_target_pairs={{0,6},{1,7},{2,0},{3,1},{4,2},{5,3},{6,4},{7,5},{8,14},{9,15},{10,... | collective-permute-start | bytes 491528 | tf_op jit(solution)/shard_map/ppermute | solution.py:191
  28.4 16.2 %collective-permute-start.4 = (bf16[32,2560]{1,0:T(8,128)(2,1)S(1)}, bf16[32,2560]{1,0:T(8,128)(2,1)S(1)}, u32[]{:S(2)}, u32[]{:S(2)}) collective-permute-start(bf16[32,2560]{1,0:T(8,128)(2,1)S(1)} %constant_dynamic-update-slice_fusion.x0.refs_0_), channel_id=1, source_target_pairs={{0,4},{1,5},{2,6},{3,7},{4,0},{5,1},{6,2},{7,3},{8,12},{9,13},{10,... | collective-permute-start | bytes 491528 | tf_op jit(solution)/shard_map/ppermute | solution.py:191
  30.4 14.2 %copy-start = (bf16[2560,320]{0,1:T(8,128)(2,1)S(1)}, bf16[2560,320]{0,1:T(8,128)(2,1)}, u32[]{:S(2)}) copy-start(bf16[2560,320]{0,1:T(8,128)(2,1)} %param.7) | copy-start | bytes 4915204
  33.2 16.5 %collective-permute-start.3 = (bf16[64,2560]{1,0:T(8,128)(2,1)S(1)}, bf16[64,2560]{1,0:T(8,128)(2,1)S(1)}, u32[]{:S(2)}, u32[]{:S(2)}) collective-permute-start(bf16[64,2560]{1,0:T(8,128)(2,1)S(1)} %get-tuple-element.38), channel_id=1, source_target_pairs={{0,1},{1,2},{2,3},{3,4},{4,5},{5,6},{6,7},{7,0},{8,9},{9,10},{10,1... | collective-permute-start | bytes 983048 | tf_op jit(solution)/shard_map/ppermute | solution.py:191
  37.2 13.1 %collective-permute-start.5 = (bf16[64,2560]{1,0:T(8,128)(2,1)S(1)}, bf16[64,2560]{1,0:T(8,128)(2,1)S(1)}, u32[]{:S(2)}, u32[]{:S(2)}) collective-permute-start(bf16[64,2560]{1,0:T(8,128)(2,1)S(1)} %get-tuple-element.44), channel_id=1, source_target_pairs={{0,7},{1,0},{2,1},{3,2},{4,3},{5,4},{6,5},{7,6},{8,15},{9,8},{10,9... | collective-permute-start | bytes 983048 | tf_op jit(solution)/shard_map/ppermute | solution.py:191
  46.4 13.0 %collective-permute-start.8 = (bf16[32,2560]{1,0:T(8,128)(2,1)S(1)}, bf16[32,2560]{1,0:T(8,128)(2,1)S(1)}, u32[]{:S(2)}, u32[]{:S(2)}) collective-permute-start(bf16[32,2560]{1,0:T(8,128)(2,1)S(1)} %get-tuple-element.48), channel_id=1, source_target_pairs={{0,4},{1,5},{2,6},{3,7},{4,0},{5,1},{6,2},{7,3},{8,12},{9,13},{10,... | collective-permute-start | bytes 491528 | tf_op jit(solution)/shard_map/ppermute | solution.py:191
  52.1 14.7 %collective-permute-start.6 = (bf16[64,2560]{1,0:T(8,128)(2,1)S(1)}, bf16[64,2560]{1,0:T(8,128)(2,1)S(1)}, u32[]{:S(2)}, u32[]{:S(2)}) collective-permute-start(bf16[64,2560]{1,0:T(8,128)(2,1)S(1)} %get-tuple-element.46), channel_id=1, source_target_pairs={{0,1},{1,2},{2,3},{3,4},{4,5},{5,6},{6,7},{7,0},{8,9},{9,10},{10,1... | collective-permute-start | bytes 983048 | tf_op jit(solution)/shard_map/ppermute | solution.py:191
  55.8 11.0 %collective-permute-start.7 = (bf16[64,2560]{1,0:T(8,128)(2,1)S(1)}, bf16[64,2560]{1,0:T(8,128)(2,1)S(1)}, u32[]{:S(2)}, u32[]{:S(2)}) collective-permute-start(bf16[64,2560]{1,0:T(8,128)(2,1)S(1)} %get-tuple-element.47), channel_id=1, source_target_pairs={{0,7},{1,0},{2,1},{3,2},{4,3},{5,4},{6,5},{7,6},{8,15},{9,8},{10,9... | collective-permute-start | bytes 983048 | tf_op jit(solution)/shard_map/ppermute | solution.py:191
  66.9 9.9 %collective-permute-start.9 = (bf16[32,2560]{1,0:T(8,128)(2,1)S(1)}, bf16[32,2560]{1,0:T(8,128)(2,1)S(1)}, u32[]{:S(2)}, u32[]{:S(2)}) collective-permute-start(bf16[32,2560]{1,0:T(8,128)(2,1)S(1)} %get-tuple-element.51), channel_id=1, source_target_pairs={{0,2},{1,3},{2,4},{3,5},{4,6},{5,7},{6,0},{7,1},{8,10},{9,11},{10,... | collective-permute-start | bytes 491528 | tf_op jit(solution)/shard_map/ppermute | solution.py:191
  69.1 9.2 %collective-permute-start.10 = (bf16[32,2560]{1,0:T(8,128)(2,1)S(1)}, bf16[32,2560]{1,0:T(8,128)(2,1)S(1)}, u32[]{:S(2)}, u32[]{:S(2)}) collective-permute-start(bf16[32,2560]{1,0:T(8,128)(2,1)S(1)} %get-tuple-element.52), channel_id=1, source_target_pairs={{0,6},{1,7},{2,0},{3,1},{4,2},{5,3},{6,4},{7,5},{8,14},{9,15},{10,... | collective-permute-start | bytes 491528 | tf_op jit(solution)/shard_map/ppermute | solution.py:191
